TPU v7x, 32 devices: a whole 2x2x4 slice. The times are simulated.
32 devices in a mesh: slab: 8 (over z, y), yz: 4 (over x, core).
Axes of the slice: x: 2, y: 2, z: 4, core: 2. Of those that a mesh axis runs over, the one named last changes fastest.
Arguments:
- grid_field: bfloat16 [32, 16, 256, 256], P(None, 'slab', 'yz'), may hold values from -6 to 6
- spectral_weight: bfloat16 [2, 32, 32, 8192], P(None, None, None, ('slab', 'yz')), may hold values from -24 to 24
- local_weight: bfloat16 [32, 32], replicated, may hold values from -1 to 1
Outputs:
- grad_field: bfloat16 [32, 16, 256, 256], P(None, 'slab', 'yz')
- grad_weight: float32 [2, 32, 32, 8192], P(None, None, None, ('slab', 'yz'))
All inputs are finite; a program needn't handle non-finite values.
Results may differ from a plain program's by a relative error of at most 0.0075.
Values sent between devices are 32-bit elements; how exact they have to be, the bound alone decides.
No kernel may reach another device: no remote copies, remote signals or barrier semaphores. Data moves between devices by JAX's collectives and lax.ppermute only.
A program may use at most 64 MiB of HBM per device.

v0:
```python
import math

import jax
import jax.numpy as jnp
import ml_dtypes
import numpy as np
from jax import lax
from jax.experimental import pallas as pl
from jax.experimental.pallas import tpu as pltpu
from jax.sharding import PartitionSpec as P

KX = 16
KY = 16
MZ = 32
NY = 256
NZ = 256
ROWS = 16

GELU_SCALE = 0.7978845608028654
GELU_CUBIC = 0.044715
BF16 = ml_dtypes.bfloat16


def freqs(number, length):
    index = np.arange(number)
    return np.where(index < number // 2, index, length - number + index)


def angles(positions, frequencies, length):
    phase = (positions[:, None].astype(np.int64) * frequencies[None, :]) % length
    return phase * (2.0 * math.pi / length)


def halves(matrix):
    matrix = np.asarray(matrix, np.float32)
    upper = matrix.astype(BF16)
    lower = (matrix - upper.astype(np.float32)).astype(BF16)
    return upper, lower


def depth_freqs(pencils):
    groups = MZ // pencils
    return np.array([[g * pencils + q for g in range(groups)] for q in range(pencils)])


def depth_analysis(pencils, doubled):
    kz = depth_freqs(pencils)
    theta = angles(kz.reshape(-1), np.arange(NZ), NZ).reshape(pencils, -1, NZ)
    weight = np.where(kz == 0, 1.0, 2.0 if doubled else 1.0)[:, :, None]
    table = np.stack([np.cos(theta) * weight, -np.sin(theta) * weight], axis=1)
    return np.concatenate(halves(table.reshape(2 * MZ, NZ)), axis=0)


def depth_synthesis(pencils, doubled):
    kz = depth_freqs(pencils)
    theta = angles(kz.reshape(-1), np.arange(NZ), NZ).reshape(pencils, -1, NZ)
    weight = np.where(kz == 0, 1.0, 2.0 if doubled else 1.0)[:, :, None]
    table = np.stack([np.cos(theta) * weight, -np.sin(theta) * weight], axis=1)
    upper, lower = halves(table.reshape(2 * MZ, NZ))
    return np.stack(
        [np.concatenate([upper, upper], 0), np.concatenate([lower, np.zeros_like(lower)], 0)]
    )


def row_analysis(pencils, planes):
    rows = NY // pencils
    tables = []
    for member in range(pencils):
        theta = angles(freqs(KY, NY), member * rows + np.arange(rows), NY)
        table = np.zeros((KY, 2, planes, 2, planes, rows))
        for x in range(planes):
            table[:, 0, x, 0, x] = np.cos(theta)
            table[:, 0, x, 1, x] = np.sin(theta)
            table[:, 1, x, 0, x] = -np.sin(theta)
            table[:, 1, x, 1, x] = np.cos(theta)
        table = table.reshape(KY * 2 * planes, 2 * planes * rows)
        tables.append(np.concatenate(halves(table), axis=0))
    return np.stack(tables)


def row_synthesis(pencils, planes):
    rows = NY // pencils
    tables = []
    for member in range(pencils):
        theta = angles(freqs(KY, NY), member * rows + np.arange(rows), NY)
        table = np.zeros((KY, 2, planes, 2, planes, rows))
        for x in range(planes):
            table[:, 0, x, 0, x] = np.cos(theta)
            table[:, 1, x, 0, x] = -np.sin(theta)
            table[:, 0, x, 1, x] = np.sin(theta)
            table[:, 1, x, 1, x] = np.cos(theta)
        upper, lower = halves(table.reshape(KY * 2 * planes, 2 * planes * rows))
        tables.append(np.concatenate([upper, upper, lower], axis=0))
    return np.stack(tables)


def plane_analysis(slabs, planes, kyn, scale):
    theta = angles(np.arange(slabs * planes), freqs(KX, slabs * planes), slabs * planes)
    theta = theta.reshape(slabs, planes, KX)
    table = np.zeros((slabs, kyn, 2, planes, 2, kyn, KX))
    for k in range(kyn):
        table[:, k, 0, :, 0, k] = np.cos(theta)
        table[:, k, 1, :, 0, k] = np.sin(theta)
        table[:, k, 0, :, 1, k] = -np.sin(theta)
        table[:, k, 1, :, 1, k] = np.cos(theta)
    upper, lower = halves(scale * table.reshape(slabs * kyn * 2 * planes, 2 * kyn * KX))
    return np.stack(
        [np.concatenate([upper, upper], 0), np.concatenate([lower, np.zeros_like(lower)], 0)]
    )


def plane_synthesis(slabs, planes, kyn, scale):
    theta = angles(np.arange(slabs * planes), freqs(KX, slabs * planes), slabs * planes)
    theta = theta.reshape(slabs, planes, KX)
    table = np.zeros((slabs, kyn, 2, planes, 2, kyn, KX))
    for k in range(kyn):
        table[:, k, 0, :, 0, k] = np.cos(theta)
        table[:, k, 0, :, 1, k] = -np.sin(theta)
        table[:, k, 1, :, 0, k] = np.sin(theta)
        table[:, k, 1, :, 1, k] = np.cos(theta)
    return np.stack(halves(scale * table.reshape(slabs * kyn * 2 * planes, 2 * kyn * KX)))


def channel_swap(channels, groups):
    table = np.zeros((groups, channels, channels, groups))
    for g in range(groups):
        for c in range(channels):
            table[g, c, c, g] = 1.0
    return table.reshape(groups * channels, channels * groups).astype(BF16)


def split(value):
    upper = value.astype(jnp.bfloat16)
    return upper, (value - upper.astype(jnp.float32)).astype(jnp.bfloat16)


def dot(left, right, left_dim=1, right_dim=0):
    return lax.dot_general(
        left, right, (((left_dim,), (right_dim,)), ((), ())), preferred_element_type=jnp.float32
    )


def analyze(grid_ref, depth_ref, row_ref, upper_ref, lower_ref, out_ref):
    channels, planes, rows, cells = grid_ref.shape
    slabs, pencils, chunk, _ = out_ref.shape
    groups = MZ // pencils
    width = planes * rows
    for c in range(0, channels, 2):
        block = grid_ref[c : c + 2].reshape(2 * width, cells)
        depth = dot(depth_ref[...], block, 1, 1)
        depth = depth[: 2 * MZ] + depth[2 * MZ :]
        for q in range(pencils):
            lines = []
            for e in range(2):
                base = q * 2 * groups
                lines.append(
                    jnp.concatenate(
                        [
                            depth[base : base + groups, e * width : (e + 1) * width],
                            depth[base + groups : base + 2 * groups, e * width : (e + 1) * width],
                        ],
                        axis=1,
                    )
                )
            upper, lower = split(jnp.concatenate(lines, axis=0))
            upper_ref[q, c * groups : (c + 2) * groups] = upper
            lower_ref[q, c * groups : (c + 2) * groups] = lower
    count = KY * 2 * planes
    for q in range(pencils):
        both = dot(row_ref[...], upper_ref[q], 1, 1)
        total = both[:count] + both[count:] + dot(row_ref[:count], lower_ref[q], 1, 1)
        out_ref[:, q] = total.reshape(slabs, chunk, channels * groups)


def analyze_kernel(grid_ref, depth_ref, row_ref, out_ref, upper_ref, lower_ref):
    analyze(grid_ref, depth_ref, row_ref, upper_ref, lower_ref, out_ref)


def collect(sums_ref, plane_ref, swap_ref, kyn):
    slabs, pencils, chunk, width = sums_ref.shape
    summed = sums_ref[:, 0]
    for member in range(1, pencils):
        summed = summed + sums_ref[:, member]
    summed = summed.reshape(slabs * chunk, width)
    stacked = jnp.concatenate(split(summed), axis=0)
    turned = dot(swap_ref[...], stacked, 1, 1).astype(jnp.bfloat16)
    coef = dot(turned, plane_ref[0]) + dot(turned, plane_ref[1])
    groups = chunk_groups(width, swap_ref)
    channels = width // groups
    parts = []
    for part in range(2):
        pieces = []
        for k in range(kyn):
            start = (part * kyn + k) * KX
            for g in range(groups):
                pieces.append(coef[g * channels : (g + 1) * channels, start : start + KX])
        parts.append(jnp.concatenate(pieces, axis=1) if len(pieces) > 1 else pieces[0])
    return parts


def chunk_groups(width, swap_ref):
    return width // CHANNELS


CHANNELS = 32


def distribute(real, imag, plane_ref, swap_ref, kyn, out_ref):
    slabs, pencils, chunk, width = out_ref.shape
    channels = real.shape[0]
    groups = width // channels
    lines = []
    for g in range(groups):
        pieces = []
        for value in (real, imag):
            for k in range(kyn):
                start = (k * groups + g) * KX
                pieces.append(value[:, start : start + KX])
        lines.append(jnp.concatenate(pieces, axis=1))
    upper, lower = split(jnp.concatenate(lines, axis=0))
    planes = (
        dot(plane_ref[0], upper, 1, 1)
        + dot(plane_ref[1], upper, 1, 1)
        + dot(plane_ref[0], lower, 1, 1)
    )
    stacked = jnp.concatenate(split(planes), axis=0)
    turned = dot(stacked, swap_ref[...])
    total = turned[: slabs * chunk] + turned[slabs * chunk :]
    total = total.reshape(slabs, chunk, width)
    for member in range(pencils):
        out_ref[:, member] = total


def mix_kernel(kyn, sums_ref, weight_ref, ahead_ref, back_ref, swap_ref, out_ref, coef_ref, mixed_ref):
    real, imag = collect(sums_ref, ahead_ref, swap_ref, kyn)
    coef_ref[0] = real
    coef_ref[1] = imag
    for o in range(weight_ref.shape[1]):
        weight_real = weight_ref[0, o].astype(jnp.float32)
        weight_imag = weight_ref[1, o].astype(jnp.float32)
        mixed_ref[0, o : o + 1] = jnp.sum(
            weight_real * real - weight_imag * imag, axis=0, keepdims=True
        )
        mixed_ref[1, o : o + 1] = jnp.sum(
            weight_real * imag + weight_imag * real, axis=0, keepdims=True
        )
    distribute(mixed_ref[0], mixed_ref[1], back_ref, swap_ref, kyn, out_ref)


def unmix_kernel(kyn, sums_ref, weight_ref, ahead_ref, back_ref, swap_ref, out_ref, coef_ref):
    real, imag = collect(sums_ref, ahead_ref, swap_ref, kyn)
    coef_ref[0] = real
    coef_ref[1] = imag
    modes_real = jnp.zeros_like(real)
    modes_imag = jnp.zeros_like(real)
    for o in range(weight_ref.shape[1]):
        weight_real = weight_ref[0, o].astype(jnp.float32)
        weight_imag = weight_ref[1, o].astype(jnp.float32)
        back_real = coef_ref[0, o : o + 1]
        back_imag = coef_ref[1, o : o + 1]
        modes_real = modes_real + (weight_real * back_real + weight_imag * back_imag)
        modes_imag = modes_imag + (weight_real * back_imag - weight_imag * back_real)
    distribute(modes_real, modes_imag, back_ref, swap_ref, kyn, out_ref)


def outer_kernel(coef_ref, back_ref, out_ref):
    real, imag = coef_ref[0], coef_ref[1]
    for o in range(back_ref.shape[1]):
        back_real = back_ref[0, o : o + 1]
        back_imag = back_ref[1, o : o + 1]
        out_ref[0, o] = back_real * real + back_imag * imag
        out_ref[1, o] = back_imag * real - back_real * imag


def lift(values_ref, row_ref, spread_ref):
    slabs, pencils, chunk, width = values_ref.shape
    groups = MZ // pencils
    channels = width // groups
    lines = []
    for q in range(pencils):
        value = values_ref[:, q].reshape(slabs * chunk, width)
        upper, lower = split(value)
        stacked = jnp.concatenate([upper, lower, upper], axis=0)
        lines.append(dot(stacked, row_ref[...], 0, 0))
    lanes = lines[0].shape[1] // 2
    for o in range(channels):
        pieces = []
        for q in range(pencils):
            for part in range(2):
                pieces.append(
                    lines[q][o * groups : (o + 1) * groups, part * lanes : (part + 1) * lanes]
                )
        block = jnp.concatenate(pieces, axis=0)
        upper = block.astype(jnp.bfloat16).astype(jnp.float32)
        both = jnp.concatenate([upper, block - upper], axis=0)
        spread_ref[o * lanes : (o + 1) * lanes] = both.T.astype(jnp.bfloat16)


def tile_sums(spread_ref, grid_ref, depth_ref, local_ref, x, y):
    channels, planes, rows, cells = grid_ref.shape
    block = grid_ref[:, x, pl.ds(y, ROWS)].reshape(channels * ROWS, cells)
    spread = spread_ref[:, x, pl.ds(y, ROWS)].reshape(channels * ROWS, 4 * MZ)
    return dot(local_ref[...], block) + dot(spread, depth_ref[0]) + dot(spread, depth_ref[1])


def middle_kernel(
    values_ref, grid_ref, local_ref, lift_ref, synth_ref, depth_ref, row_ref,
    up_ref, out_ref, spread_ref, upper_ref, lower_ref,
):
    channels, planes, rows, cells = grid_ref.shape
    lift(values_ref, lift_ref, spread_ref)
    spread = spread_ref.reshape(channels, planes, rows, 4 * MZ)

    def step(index, carry):
        x = index // (rows // ROWS)
        y = pl.multiple_of((index % (rows // ROWS)) * ROWS, ROWS)
        before = tile_sums(spread, grid_ref, synth_ref, local_ref, x, y)
        square = before * before
        inner = before * (GELU_SCALE + (GELU_SCALE * GELU_CUBIC) * square)
        gate = 0.5 + 0.5 * jnp.tanh(inner)
        twice = 2.0 * GELU_SCALE + (6.0 * GELU_SCALE * GELU_CUBIC) * square
        slope = 1.0 + before * (1.0 - gate) * twice
        upstream = (before * gate) * (gate * slope)
        up_ref[:, x, pl.ds(y, ROWS)] = upstream.astype(jnp.bfloat16).reshape(channels, ROWS, cells)
        return carry

    lax.fori_loop(0, planes * (rows // ROWS), step, 0)
    analyze(up_ref, depth_ref, row_ref, upper_ref, lower_ref, out_ref)


def final_kernel(values_ref, grid_ref, local_ref, lift_ref, synth_ref, out_ref, spread_ref):
    channels, planes, rows, cells = grid_ref.shape
    lift(values_ref, lift_ref, spread_ref)
    spread = spread_ref.reshape(channels, planes, rows, 4 * MZ)

    def step(index, carry):
        x = index // (rows // ROWS)
        y = pl.multiple_of((index % (rows // ROWS)) * ROWS, ROWS)
        total = tile_sums(spread, grid_ref, synth_ref, local_ref, x, y)
        out_ref[:, x, pl.ds(y, ROWS)] = total.astype(jnp.bfloat16).reshape(channels, ROWS, cells)
        return carry

    lax.fori_loop(0, planes * (rows // ROWS), step, 0)


VMEM = pl.BlockSpec(memory_space=pltpu.VMEM)


def call(kernel, outs, scratch, *operands, flops=1 << 30, size=4 << 20):
    return pl.pallas_call(
        kernel,
        out_shape=outs,
        in_specs=[VMEM] * len(operands),
        out_specs=jax.tree.map(lambda _: VMEM, outs),
        scratch_shapes=scratch,
        compiler_params=pltpu.CompilerParams(vmem_limit_bytes=40 << 20),
        cost_estimate=pl.CostEstimate(flops=flops, bytes_accessed=size, transcendentals=0),
    )(*operands)


def f32(*shape):
    return jax.ShapeDtypeStruct(shape, jnp.float32)


def bf16(*shape):
    return jax.ShapeDtypeStruct(shape, jnp.bfloat16)


def on_device(grid_field, spectral_weight, local_weight):
    channels, planes, rows, cells = grid_field.shape
    slabs = lax.axis_size("slab")
    pencils = lax.axis_size("yz")
    groups = MZ // pencils
    member = lax.axis_index("yz")
    scale = 1.0 / math.sqrt(planes * slabs * NY * NZ)
    pairs = KY * groups // slabs
    kyn = max(1, pairs // groups)
    gn = pairs // kyn
    blocks = KY // kyn
    turns = groups // gn
    lanes = channels * groups
    line = kyn * 2 * planes
    modes = spectral_weight.shape[3]

    row_ahead = lax.dynamic_index_in_dim(jnp.asarray(row_analysis(pencils, planes)), member, 0, False)
    row_back = lax.dynamic_index_in_dim(jnp.asarray(row_synthesis(pencils, planes)), member, 0, False)
    plane_ahead = jnp.asarray(plane_analysis(slabs, planes, kyn, scale))
    plane_back = jnp.asarray(plane_synthesis(slabs, planes, kyn, scale))
    swap = jnp.asarray(channel_swap(channels, gn))
    repeat = jnp.asarray(np.repeat(np.eye(channels), ROWS, axis=0).astype(BF16))
    mask = jnp.asarray(np.tile(np.eye(ROWS), (channels, channels)).astype(BF16))

    def widen(weight):
        rows_wide = dot(repeat, weight).astype(jnp.bfloat16)
        return dot(rows_wide, repeat, 1, 1).astype(jnp.bfloat16) * mask

    def to_owner(parts):
        if turns > 1:
            parts = parts.reshape(blocks, pencils, line, channels, turns, gn)
            parts = jnp.transpose(parts, (0, 4, 1, 2, 3, 5))
        parts = parts.reshape(slabs * pencils, line, channels * gn)
        moved = lax.all_to_all(parts, ("slab", "yz"), 0, 0, tiled=True)
        return moved.reshape(slabs, pencils, line, channels * gn)

    def from_owner(values):
        values = values.reshape(slabs * pencils, line, channels * gn)
        moved = lax.all_to_all(values, ("slab", "yz"), 0, 0, tiled=True)
        if turns > 1:
            moved = moved.reshape(blocks, turns, pencils, line, channels, gn)
            moved = jnp.transpose(moved, (0, 2, 3, 4, 1, 5))
        return moved.reshape(blocks, pencils, line, lanes)

    halves_scratch = [pltpu.VMEM((pencils, lanes, 2 * planes * rows), jnp.bfloat16)] * 2
    spread_scratch = pltpu.VMEM((channels * planes * rows, 4 * MZ), jnp.bfloat16)
    sent = f32(blocks, pencils, line, lanes)
    given = f32(slabs, pencils, line, channels * gn)
    coefs = f32(2, channels, modes)

    parts = call(
        analyze_kernel, sent, halves_scratch,
        grid_field, jnp.asarray(depth_analysis(pencils, False)), row_ahead,
    )
    received = to_owner(parts)

    def mix(*refs):
        mix_kernel(kyn, *refs)

    values, coef = call(
        mix, (given, coefs), [pltpu.VMEM((2, channels, modes), jnp.float32)],
        received, spectral_weight, plane_ahead, plane_back, swap,
    )
    upstream, parts = call(
        middle_kernel,
        (bf16(channels, planes, rows, cells), sent),
        [spread_scratch] + halves_scratch,
        from_owner(values), grid_field, widen(local_weight), row_back,
        jnp.asarray(depth_synthesis(pencils, True)), jnp.asarray(depth_analysis(pencils, True)), row_ahead,
    )
    received = to_owner(parts)

    def unmix(*refs):
        unmix_kernel(kyn, *refs)

    values, back = call(
        unmix, (given, coefs), [],
        received, spectral_weight, plane_ahead, plane_back, swap,
    )
    grad_weight = call(outer_kernel, f32(2, channels, channels, modes), [], coef, back)
    grad_field = call(
        final_kernel, bf16(channels, planes, rows, cells), [spread_scratch],
        from_owner(values), upstream, widen(local_weight.T), row_back,
        jnp.asarray(depth_synthesis(pencils, False)),
    )
    return grad_field, grad_weight


def solution(mesh):
    return jax.shard_map(
        on_device,
        mesh=mesh,
        in_specs=(P(None, "slab", "yz", None), P(None, None, None, ("slab", "yz")), P()),
        out_specs=(P(None, "slab", "yz", None), P(None, None, None, ("slab", "yz"))),
        check_vma=False,
    )
```

profile of v0, /device:TPU:0, one launch (start us, length us, event | category | flops | bytes accessed | tf_op | source)
XLA Modules:
  0.0 80.4 jit_solution(8341596019602674533)
XLA Ops:
  0.6 0.0 copy-start
  0.6 0.9 %dynamic-slice_bitcast_fusion.1.row_ref = bf16[128,256]{1,0:T(8,128)(2,1)S(1)} fusion(bf16[4,128,256]{2,1,0:T(8,128)(2,1)} %constant.36.clone, s32[]{:T(128)S(6)} %select_n.6), kind=kLoop, calls=%fused_computation.7 | loop fusion | bytes 131076 | tf_op jit(solution)/shard_map/jit(dynamic_index_in_dim)/squeeze | solution.py:385
  1.5 1.6 %copy-done.2 = bf16[32,2,64,256]{3,2,1,0:T(8,128)(2,1)S(1)} copy-done((bf16[32,2,64,256]{3,2,1,0:T(8,128)(2,1)S(1)}, bf16[32,2,64,256]{3,2,1,0:T(8,128)(2,1)}, u32[]{:S(2)}) %copy-start.2) | copy-done | bytes 2097176
  3.1 0.8 %copy-done.10 = bf16[128,256]{1,0:T(8,128)(2,1)S(1)} copy-done((bf16[128,256]{1,0:T(8,128)(2,1)S(1)}, bf16[128,256]{1,0:T(8,128)(2,1)}, u32[]{:S(2)}) %copy-start.10) | copy-done | bytes 65560
  3.9 1.2 %shard_map.149 = f32[8,4,8,256]{3,2,1,0:T(8,128)S(1)} custom-call(bf16[32,2,64,256]{3,2,1,0:T(8,128)(2,1)S(1)} %copy-done.2, bf16[128,256]{1,0:T(8,128)(2,1)S(1)} %copy-done.10, bf16[128,256]{1,0:T(8,128)(2,1)S(1)} %dynamic-slice_bitcast_fusion.1.row_ref), custom_call_target="tpu_custom_call" | custom-call | flops 1073741824 | bytes 4194304 | tf_op jit(solution)/shard_map/pallas_call | solution.py:350
  5.1 17.7 %all_to_all.20 = f32[32,8,256]{2,1,0:T(8,128)S(1)} all-to-all(f32[32,8,256]{2,1,0:T(8,128)S(1)} %bitcast.23), channel_id=1, replica_groups=mesh['slab'=8,'yz'=4] {'slab','yz'}, dimensions={0} | all-to-all | bytes 524288 | tf_op jit(solution)/shard_map/all_to_all | solution.py:402
  22.8 0.0 copy-done.4
  22.8 0.0 copy-done.6
  22.8 0.0 copy-done.8
  22.8 0.0 copy-done.11
  22.9 0.0 copy-start.12
  22.9 0.0 copy-start.7
  22.9 0.0 copy-start.9
  22.9 2.3 %shard_map.150 = (f32[8,4,8,256]{3,2,1,0:T(8,128)}, f32[2,32,256]{2,1,0:T(8,128)S(1)}) custom-call(f32[8,4,8,256]{3,2,1,0:T(8,128)S(1)} %bitcast.22, bf16[2,32,32,256]{3,2,1,0:T(8,128)(2,1)S(1)} %copy-done.4, bf16[2,128,64]{2,1,0:T(8,128)(2,1)S(1)} %copy-done.8, bf16[2,64,64]{2,1,0:T(8,128)(2,1)S(1)} %copy-done.11, bf16[256,256]{1,0:T(8,128)(2,1)S(1)} %copy-done.6), custom_call_target="tpu_custom_call" | custom-call | flops 1073741824 | bytes 4194304 | tf_op jit(solution)/shard_map/pallas_call | solution.py:350
  25.2 2.6 %all-to-all-start.1 = ((f32[32,8,256]{2,1,0:T(8,128)}), f32[32,8,256]{2,1,0:T(8,128)S(1)}, u32[]{:S(2)}, u32[]{:S(2)}) async-start(f32[32,8,256]{2,1,0:T(8,128)} %bitcast.3), calls=%async_computation.1 | async-start | bytes 524288 | tf_op jit(solution)/shard_map/all_to_all | solution.py:407
  27.7 0.9 %dynamic-slice_bitcast_fusion.lift_ref = bf16[192,256]{1,0:T(8,128)(2,1)S(1)} fusion(bf16[4,192,256]{2,1,0:T(8,128)(2,1)} %constant.37.clone, s32[]{:T(128)S(6)} %select_n.6), kind=kLoop, calls=%fused_computation.6 | loop fusion | bytes 196612 | tf_op jit(solution)/shard_map/jit(dynamic_index_in_dim)/squeeze | solution.py:386
  28.7 0.0 copy-done
  28.7 1.4 %fusion.local_ref = bf16[512,512]{1,0:T(8,128)(2,1)S(1)} fusion(bf16[512,512]{1,0:T(8,128)(2,1)} %constant.42.clone, bf16[512,32]{1,0:T(8,128)(2,1)S(1)} %copy-done.12, bf16[32,32]{1,0:T(8,128)(2,1)S(1)} %copy-done), kind=kOutput, calls=%fused_computation.2 | convolution fusion | flops 19152896 | bytes 1083392 | tf_op jit(solution)/shard_map/dot_general | solution.py:138
  30.1 8.2 %all-to-all-done.1 = f32[32,8,256]{2,1,0:T(8,128)S(1)} async-done(((f32[32,8,256]{2,1,0:T(8,128)}), f32[32,8,256]{2,1,0:T(8,128)S(1)}, u32[]{:S(2)}, u32[]{:S(2)}) %all-to-all-start.1) | async-done | bytes 262176 | tf_op jit(solution)/shard_map/all_to_all | solution.py:407
  38.3 0.0 copy-done.9
  38.4 1.6 %copy-done.3 = bf16[32,2,64,256]{3,2,1,0:T(8,128)(2,1)S(1)} copy-done((bf16[32,2,64,256]{3,2,1,0:T(8,128)(2,1)S(1)}, bf16[32,2,64,256]{3,2,1,0:T(8,128)(2,1)}, u32[]{:S(2)}) %copy-start.3) | copy-done | bytes 2097176
  39.9 6.9 %shard_map.151 = (bf16[32,2,64,256]{3,2,1,0:T(8,128)(2,1)S(1)}, f32[8,4,8,256]{3,2,1,0:T(8,128)S(1)}) custom-call(f32[8,4,8,256]{3,2,1,0:T(8,128)S(1)} %bitcast.19, bf16[32,2,64,256]{3,2,1,0:T(8,128)(2,1)S(1)} %copy-done.3, bf16[512,512]{1,0:T(8,128)(2,1)S(1)} %fusion.local_ref, bf16[192,256]{1,0:T(8,128)(2,1)S(1)} %dynamic-slice_bitcast_fusion.lift_ref, ...), custom_call_target="tpu_custom_call" | custom-call | flops 1073741824 | bytes 4194304 | tf_op jit(solution)/shard_map/pallas_call | solution.py:350
  46.8 12.7 %all_to_all.21 = f32[32,8,256]{2,1,0:T(8,128)S(1)} all-to-all(f32[32,8,256]{2,1,0:T(8,128)S(1)} %bitcast.20), channel_id=1, replica_groups=mesh['slab'=8,'yz'=4] {'slab','yz'}, dimensions={0} | all-to-all | bytes 524288 | tf_op jit(solution)/shard_map/all_to_all | solution.py:402
  59.5 2.2 %shard_map.152 = (f32[8,4,8,256]{3,2,1,0:T(8,128)}, f32[2,32,256]{2,1,0:T(8,128)S(1)}) custom-call(f32[8,4,8,256]{3,2,1,0:T(8,128)S(1)} %bitcast.21, bf16[2,32,32,256]{3,2,1,0:T(8,128)(2,1)S(1)} %copy-done.5, bf16[2,128,64]{2,1,0:T(8,128)(2,1)S(1)} %copy-done.8, bf16[2,64,64]{2,1,0:T(8,128)(2,1)S(1)} %copy-done.11, bf16[256,256]{1,0:T(8,128)(2,1)S(1)} %copy-done.6), custom_call_target="tpu_custom_call" | custom-call | flops 1073741824 | bytes 4194304 | tf_op jit(solution)/shard_map/pallas_call | solution.py:350
  61.7 2.6 %all-to-all-start.3 = ((f32[32,8,256]{2,1,0:T(8,128)}), f32[32,8,256]{2,1,0:T(8,128)S(1)}, u32[]{:S(2)}, u32[]{:S(2)}) async-start(f32[32,8,256]{2,1,0:T(8,128)} %bitcast.8), calls=%async_computation.3 | async-start | bytes 524288 | tf_op jit(solution)/shard_map/all_to_all | solution.py:407
  64.3 0.0 copy-done.13
  64.3 1.4 %fusion.1.local_ref = bf16[512,512]{1,0:T(8,128)(2,1)S(1)} fusion(bf16[512,512]{1,0:T(8,128)(2,1)} %constant.42.clone, bf16[512,32]{1,0:T(8,128)(2,1)S(1)} %copy-done.13, bf16[32,32]{1,0:T(8,128)(2,1)S(1)} %copy-done), kind=kOutput, calls=%fused_computation.3 | convolution fusion | flops 19152896 | bytes 1083392 | tf_op jit(solution)/shard_map/dot_general | solution.py:138
  65.8 0.0 copy-start.1
  65.8 1.5 %shard_map.154 = f32[2,32,32,256]{3,2,1,0:T(8,128)} custom-call(f32[2,32,256]{2,1,0:T(8,128)S(1)} %get-tuple-element.12.coef_ref, f32[2,32,256]{2,1,0:T(8,128)S(1)} %get-tuple-element.13.back_ref), custom_call_target="tpu_custom_call" | custom-call | flops 1073741824 | bytes 4194304 | tf_op jit(solution)/shard_map/pallas_call | solution.py:350
  67.3 7.6 %all-to-all-done.3 = f32[32,8,256]{2,1,0:T(8,128)S(1)} async-done(((f32[32,8,256]{2,1,0:T(8,128)}), f32[32,8,256]{2,1,0:T(8,128)S(1)}, u32[]{:S(2)}, u32[]{:S(2)}) %all-to-all-start.3) | async-done | bytes 262176 | tf_op jit(solution)/shard_map/all_to_all | solution.py:407
  74.9 0.0 copy-done.1
  74.9 5.4 %shard_map.153 = bf16[32,2,64,256]{3,2,1,0:T(8,128)(2,1)} custom-call(f32[8,4,8,256]{3,2,1,0:T(8,128)S(1)} %bitcast.18, bf16[32,2,64,256]{3,2,1,0:T(8,128)(2,1)S(1)} %get-tuple-element.11.grid_ref, bf16[512,512]{1,0:T(8,128)(2,1)S(1)} %fusion.1.local_ref, bf16[192,256]{1,0:T(8,128)(2,1)S(1)} %dynamic-slice_bitcast_fusion.lift_ref, ...), custom_call_target="tpu_custom_call" | custom-call | flops 1073741824 | bytes 4194304 | tf_op jit(solution)/shard_map/pallas_call | solution.py:350
  (12 shorter events, 0.0 us)
Async XLA Ops:
  0.6 28.0 %copy-start = (bf16[32,32]{1,0:T(8,128)(2,1)S(1)}, bf16[32,32]{1,0:T(8,128)(2,1)}, u32[]{:S(2)}) copy-start(bf16[32,32]{1,0:T(8,128)(2,1)} %param.16) | copy-start | bytes 6148
  1.5 1.6 %copy-start.2 = (bf16[32,2,64,256]{3,2,1,0:T(8,128)(2,1)S(1)}, bf16[32,2,64,256]{3,2,1,0:T(8,128)(2,1)}, u32[]{:S(2)}) copy-start(bf16[32,2,64,256]{3,2,1,0:T(8,128)(2,1)} %grid_ref.3) | copy-start | bytes 6291460
  3.1 0.8 %copy-start.10 = (bf16[128,256]{1,0:T(8,128)(2,1)S(1)}, bf16[128,256]{1,0:T(8,128)(2,1)}, u32[]{:S(2)}) copy-start(bf16[128,256]{1,0:T(8,128)(2,1)} %constant.43.clone.depth_ref) | copy-start | bytes 196612
  3.9 18.9 %copy-start.4 = (bf16[2,32,32,256]{3,2,1,0:T(8,128)(2,1)S(1)}, bf16[2,32,32,256]{3,2,1,0:T(8,128)(2,1)}, u32[]{:S(2)}) copy-start(bf16[2,32,32,256]{3,2,1,0:T(8,128)(2,1)} %refs_1_.3) | copy-start | bytes 3145732
  3.9 18.9 %copy-start.6 = (bf16[256,256]{1,0:T(8,128)(2,1)S(1)}, bf16[256,256]{1,0:T(8,128)(2,1)}, u32[]{:S(2)}) copy-start(bf16[256,256]{1,0:T(8,128)(2,1)} %constant.40.clone.refs_4_) | copy-start | bytes 393220
  3.9 18.9 %copy-start.8 = (bf16[2,128,64]{2,1,0:T(8,128)(2,1)S(1)}, bf16[2,128,64]{2,1,0:T(8,128)(2,1)}, u32[]{:S(2)}) copy-start(bf16[2,128,64]{2,1,0:T(8,128)(2,1)} %constant.38.clone.refs_2_) | copy-start | bytes 98308
  3.9 18.9 %copy-start.11 = (bf16[2,64,64]{2,1,0:T(8,128)(2,1)S(1)}, bf16[2,64,64]{2,1,0:T(8,128)(2,1)}, u32[]{:S(2)}) copy-start(bf16[2,64,64]{2,1,0:T(8,128)(2,1)} %constant.39.clone.refs_3_) | copy-start | bytes 49156
  22.9 5.8 %copy-start.12 = (bf16[512,32]{1,0:T(8,128)(2,1)S(1)}, bf16[512,32]{1,0:T(8,128)(2,1)}, u32[]{:S(2)}) copy-start(bf16[512,32]{1,0:T(8,128)(2,1)} %constant.41.clone) | copy-start | bytes 98308
  22.9 15.5 %copy-start.7 = (bf16[2,128,256]{2,1,0:T(8,128)(2,1)S(1)}, bf16[2,128,256]{2,1,0:T(8,128)(2,1)}, u32[]{:S(2)}) copy-start(bf16[2,128,256]{2,1,0:T(8,128)(2,1)} %constant.44.clone.synth_ref) | copy-start | bytes 393220
  22.9 15.5 %copy-start.9 = (bf16[128,256]{1,0:T(8,128)(2,1)S(1)}, bf16[128,256]{1,0:T(8,128)(2,1)}, u32[]{:S(2)}) copy-start(bf16[128,256]{1,0:T(8,128)(2,1)} %constant.45.clone.depth_ref) | copy-start | bytes 196612
  25.2 13.2 %all-to-all-start.1 = ((f32[32,8,256]{2,1,0:T(8,128)}), f32[32,8,256]{2,1,0:T(8,128)S(1)}, u32[]{:S(2)}, u32[]{:S(2)}) async-start(f32[32,8,256]{2,1,0:T(8,128)} %bitcast.3), calls=%async_computation.1 | async-start | bytes 524288 | tf_op jit(solution)/shard_map/all_to_all | solution.py:407
  38.4 1.6 %copy-start.3 = (bf16[32,2,64,256]{3,2,1,0:T(8,128)(2,1)S(1)}, bf16[32,2,64,256]{3,2,1,0:T(8,128)(2,1)}, u32[]{:S(2)}) copy-start(bf16[32,2,64,256]{3,2,1,0:T(8,128)(2,1)} %grid_ref.3) | copy-start | bytes 6291460
  39.9 19.6 %copy-start.5 = (bf16[2,32,32,256]{3,2,1,0:T(8,128)(2,1)S(1)}, bf16[2,32,32,256]{3,2,1,0:T(8,128)(2,1)}, u32[]{:S(2)}) copy-start(bf16[2,32,32,256]{3,2,1,0:T(8,128)(2,1)} %refs_1_.3) | copy-start | bytes 3145732
  59.5 4.8 %copy-start.13 = (bf16[512,32]{1,0:T(8,128)(2,1)S(1)}, bf16[512,32]{1,0:T(8,128)(2,1)}, u32[]{:S(2)}) copy-start(bf16[512,32]{1,0:T(8,128)(2,1)} %constant.41.clone) | copy-start | bytes 98308
  61.7 13.2 %all-to-all-start.3 = ((f32[32,8,256]{2,1,0:T(8,128)}), f32[32,8,256]{2,1,0:T(8,128)S(1)}, u32[]{:S(2)}, u32[]{:S(2)}) async-start(f32[32,8,256]{2,1,0:T(8,128)} %bitcast.8), calls=%async_computation.3 | async-start | bytes 524288 | tf_op jit(solution)/shard_map/all_to_all | solution.py:407
  65.8 9.2 %copy-start.1 = (bf16[2,128,256]{2,1,0:T(8,128)(2,1)S(1)}, bf16[2,128,256]{2,1,0:T(8,128)(2,1)}, u32[]{:S(2)}) copy-start(bf16[2,128,256]{2,1,0:T(8,128)(2,1)} %constant.46.clone.synth_ref) | copy-start | bytes 393220
where the time goes:
time: 80.9 us; the launch traced here: 80.4 us
  blocking collectives  30.4 us (38%)
  Pallas kernels  19.5 us (24%)
  waiting for transfers between devices  15.8 us (20%)
  local copies, waits for them, and re-layouts  5.84 us (7%)
  starting transfers between devices  5.17 us (6%)
  matrix products  2.87 us (4%)
    all_to_all x2, blocking collectives, to_owner(): moved = lax.all_to_all(parts, ('slab', 'yz'), 0, 0, tiled=True)  30.4 us
    pallas_call x6, Pallas kernels, call(): pl.pallas_call(kernel, out_shape=outs, in_specs=[VMEM] * len(operands), o...  19.5 us
    all_to_all x2, waiting for transfers between devices, from_owner(): moved = lax.all_to_all(values, ('slab', 'yz'), 0, 0, tiled=True)  15.8 us
    all_to_all x2, starting transfers between devices, from_owner(): moved = lax.all_to_all(values, ('slab', 'yz'), 0, 0, tiled=True)  5.17 us
    unnamed x28, local copies, waits for them, and re-layouts  4.08 us
    dot_general x2, matrix products, dot(): lax.dot_general(left, right, (((left_dim,), (right_dim,)), ((), ())), pre...  2.87 us
  transfers between devices with their start and end apart: 2, of which 2 were waited for; matrix products, arithmetic and copies ran while one was open for 5% of the time, Pallas kernels for 2%

commit v1 on v0

--- a/solution.py
+++ b/solution.py
@@ -15,10 +15,12 @@
 NY = 256
 NZ = 256
 ROWS = 16
+PIECES = 2
 
 GELU_SCALE = 0.7978845608028654
 GELU_CUBIC = 0.044715
 BF16 = ml_dtypes.bfloat16
+LARGE = 53248
 
 
 def freqs(number, length):
@@ -56,10 +58,7 @@
     theta = angles(kz.reshape(-1), np.arange(NZ), NZ).reshape(pencils, -1, NZ)
     weight = np.where(kz == 0, 1.0, 2.0 if doubled else 1.0)[:, :, None]
     table = np.stack([np.cos(theta) * weight, -np.sin(theta) * weight], axis=1)
-    upper, lower = halves(table.reshape(2 * MZ, NZ))
-    return np.stack(
-        [np.concatenate([upper, upper], 0), np.concatenate([lower, np.zeros_like(lower)], 0)]
-    )
+    return np.tile(table.reshape(2 * MZ, NZ), (2, 1)).astype(BF16)
 
 
 def row_analysis(pencils, planes):
@@ -140,12 +139,13 @@
     )
 
 
-def analyze(grid_ref, depth_ref, row_ref, upper_ref, lower_ref, out_ref):
+def analyze(grid_ref, depth_ref, row_ref, upper_ref, lower_ref, kept_ref, sent_ref, ready):
     channels, planes, rows, cells = grid_ref.shape
-    slabs, pencils, chunk, _ = out_ref.shape
+    blocks, pencils, line, half = kept_ref.shape
     groups = MZ // pencils
     width = planes * rows
     for c in range(0, channels, 2):
+        ready(c)
         block = grid_ref[c : c + 2].reshape(2 * width, cells)
         depth = dot(depth_ref[...], block, 1, 1)
         depth = depth[: 2 * MZ] + depth[2 * MZ :]
@@ -165,28 +165,60 @@
             upper, lower = split(jnp.concatenate(lines, axis=0))
             upper_ref[q, c * groups : (c + 2) * groups] = upper
             lower_ref[q, c * groups : (c + 2) * groups] = lower
+    ready(channels)
     count = KY * 2 * planes
+    first = lax.axis_index("yz") % 2 == 0
     for q in range(pencils):
         both = dot(row_ref[...], upper_ref[q], 1, 1)
         total = both[:count] + both[count:] + dot(row_ref[:count], lower_ref[q], 1, 1)
-        out_ref[:, q] = total.reshape(slabs, chunk, channels * groups)
-
-
-def analyze_kernel(grid_ref, depth_ref, row_ref, out_ref, upper_ref, lower_ref):
-    analyze(grid_ref, depth_ref, row_ref, upper_ref, lower_ref, out_ref)
-
-
-def collect(sums_ref, plane_ref, swap_ref, kyn):
-    slabs, pencils, chunk, width = sums_ref.shape
-    summed = sums_ref[:, 0]
-    for member in range(1, pencils):
-        summed = summed + sums_ref[:, member]
-    summed = summed.reshape(slabs * chunk, width)
-    stacked = jnp.concatenate(split(summed), axis=0)
+        low = total[:, :half].reshape(blocks, line, half)
+        high = total[:, half:].reshape(blocks, line, half)
+        kept_ref[:, q] = jnp.where(first, low, high)
+        sent_ref[:, q] = jnp.where(first, high, low)
+
+
+def analyze_kernel(
+    grid_hbm, depth_hbm, row_hbm, kept_ref, sent_ref,
+    grid_ref, depth_ref, row_ref, upper_ref, lower_ref, piece_sem, table_sem,
+):
+    channels = grid_hbm.shape[0]
+    step = channels // PIECES
+    member = lax.axis_index("yz")
+    depth_copy = pltpu.make_async_copy(depth_hbm, depth_ref, table_sem.at[0])
+    row_copy = pltpu.make_async_copy(row_hbm.at[member], row_ref, table_sem.at[1])
+    pieces = [
+        pltpu.make_async_copy(
+            grid_hbm.at[pl.ds(i * step, step)], grid_ref.at[pl.ds(i * step, step)], piece_sem.at[i]
+        )
+        for i in range(PIECES)
+    ]
+    depth_copy.start()
+    for piece in pieces:
+        piece.start()
+    row_copy.start()
+    depth_copy.wait()
+
+    def ready(c):
+        if c == channels:
+            row_copy.wait()
+        elif c % step == 0:
+            pieces[c // step].wait()
+
+    analyze(grid_ref, depth_ref, row_ref, upper_ref, lower_ref, kept_ref, sent_ref, ready)
+
+
+def collect(sums_ref, plane_ref, swap_ref, kyn, channels):
+    slabs, pencils, line, half = sums_ref.shape
+    sides = []
+    for core in range(2):
+        side = sums_ref[:, core]
+        for member in range(core + 2, pencils, 2):
+            side = side + sums_ref[:, member]
+        sides.append(side.reshape(slabs * line, half))
+    stacked = jnp.concatenate(split(jnp.concatenate(sides, axis=1)), axis=0)
     turned = dot(swap_ref[...], stacked, 1, 1).astype(jnp.bfloat16)
     coef = dot(turned, plane_ref[0]) + dot(turned, plane_ref[1])
-    groups = chunk_groups(width, swap_ref)
-    channels = width // groups
+    groups = 2 * half // channels
     parts = []
     for part in range(2):
         pieces = []
@@ -198,17 +230,10 @@
     return parts
 
 
-def chunk_groups(width, swap_ref):
-    return width // CHANNELS
-
-
-CHANNELS = 32
-
-
 def distribute(real, imag, plane_ref, swap_ref, kyn, out_ref):
-    slabs, pencils, chunk, width = out_ref.shape
+    slabs, pencils, line, half = out_ref.shape
     channels = real.shape[0]
-    groups = width // channels
+    groups = 2 * half // channels
     lines = []
     for g in range(groups):
         pieces = []
@@ -225,16 +250,20 @@
     )
     stacked = jnp.concatenate(split(planes), axis=0)
     turned = dot(stacked, swap_ref[...])
-    total = turned[: slabs * chunk] + turned[slabs * chunk :]
-    total = total.reshape(slabs, chunk, width)
+    total = turned[: slabs * line] + turned[slabs * line :]
     for member in range(pencils):
-        out_ref[:, member] = total
-
-
-def mix_kernel(kyn, sums_ref, weight_ref, ahead_ref, back_ref, swap_ref, out_ref, coef_ref, mixed_ref):
-    real, imag = collect(sums_ref, ahead_ref, swap_ref, kyn)
+        side = total[:, member % 2 * half : (member % 2 + 1) * half]
+        out_ref[:, member] = side.reshape(slabs, line, half)
+
+
+def mix_kernel(
+    kyn, sums_ref, weight_ref, ahead_ref, back_ref, swap_ref, out_ref, coef_hbm, coef_ref, mixed_ref, sem
+):
+    real, imag = collect(sums_ref, ahead_ref, swap_ref, kyn, weight_ref.shape[1])
     coef_ref[0] = real
     coef_ref[1] = imag
+    copy = pltpu.make_async_copy(coef_ref, coef_hbm, sem)
+    copy.start()
     for o in range(weight_ref.shape[1]):
         weight_real = weight_ref[0, o].astype(jnp.float32)
         weight_imag = weight_ref[1, o].astype(jnp.float32)
@@ -245,10 +274,11 @@
             weight_real * imag + weight_imag * real, axis=0, keepdims=True
         )
     distribute(mixed_ref[0], mixed_ref[1], back_ref, swap_ref, kyn, out_ref)
+    copy.wait()
 
 
 def unmix_kernel(kyn, sums_ref, weight_ref, ahead_ref, back_ref, swap_ref, out_ref, coef_ref):
-    real, imag = collect(sums_ref, ahead_ref, swap_ref, kyn)
+    real, imag = collect(sums_ref, ahead_ref, swap_ref, kyn, weight_ref.shape[1])
     coef_ref[0] = real
     coef_ref[1] = imag
     modes_real = jnp.zeros_like(real)
@@ -272,13 +302,18 @@
         out_ref[1, o] = back_imag * real - back_real * imag
 
 
-def lift(values_ref, row_ref, spread_ref):
-    slabs, pencils, chunk, width = values_ref.shape
+def lift(mine_ref, other_ref, row_ref, spread_ref):
+    blocks, pencils, line, half = mine_ref.shape
     groups = MZ // pencils
-    channels = width // groups
+    channels = 2 * half // groups
+    first = lax.axis_index("yz") % 2 == 0
     lines = []
     for q in range(pencils):
-        value = values_ref[:, q].reshape(slabs * chunk, width)
+        mine = mine_ref[:, q].reshape(blocks * line, half)
+        other = other_ref[:, q].reshape(blocks * line, half)
+        value = jnp.concatenate(
+            [jnp.where(first, mine, other), jnp.where(first, other, mine)], axis=1
+        )
         upper, lower = split(value)
         stacked = jnp.concatenate([upper, lower, upper], axis=0)
         lines.append(dot(stacked, row_ref[...], 0, 0))
@@ -296,65 +331,90 @@
         spread_ref[o * lanes : (o + 1) * lanes] = both.T.astype(jnp.bfloat16)
 
 
-def tile_sums(spread_ref, grid_ref, depth_ref, local_ref, x, y):
+def tile(ref, x, y):
+    return ref[:, x, y : y + ROWS].reshape(ref.shape[0] * ROWS, ref.shape[3])
+
+
+def fetch(hbm, ref, sem):
+    copy = pltpu.make_async_copy(hbm, ref, sem)
+    copy.start()
+    return copy
+
+
+def tiles(ref):
+    for x in range(ref.shape[1]):
+        for y in range(0, ref.shape[2], ROWS):
+            yield x, y
+
+
+def local_kernel(grid_ref, wide_ref, out_ref):
     channels, planes, rows, cells = grid_ref.shape
-    block = grid_ref[:, x, pl.ds(y, ROWS)].reshape(channels * ROWS, cells)
-    spread = spread_ref[:, x, pl.ds(y, ROWS)].reshape(channels * ROWS, 4 * MZ)
-    return dot(local_ref[...], block) + dot(spread, depth_ref[0]) + dot(spread, depth_ref[1])
+    for x, y in tiles(grid_ref):
+        total = dot(wide_ref[...], tile(grid_ref, x, y))
+        out_ref[:, x, y : y + ROWS] = total.reshape(channels, ROWS, cells)
 
 
 def middle_kernel(
-    values_ref, grid_ref, local_ref, lift_ref, synth_ref, depth_ref, row_ref,
-    up_ref, out_ref, spread_ref, upper_ref, lower_ref,
+    mine_ref, other_ref, local_ref, lift_ref, synth_ref, depth_ref, row_hbm,
+    up_ref, kept_ref, sent_ref, spread_ref, row_ref, upper_ref, lower_ref, row_sem,
 ):
-    channels, planes, rows, cells = grid_ref.shape
-    lift(values_ref, lift_ref, spread_ref)
+    channels, planes, rows, cells = local_ref.shape
+    row_copy = fetch(row_hbm.at[lax.axis_index("yz")], row_ref, row_sem)
+    lift(mine_ref, other_ref, lift_ref, spread_ref)
     spread = spread_ref.reshape(channels, planes, rows, 4 * MZ)
-
-    def step(index, carry):
-        x = index // (rows // ROWS)
-        y = pl.multiple_of((index % (rows // ROWS)) * ROWS, ROWS)
-        before = tile_sums(spread, grid_ref, synth_ref, local_ref, x, y)
+    for x, y in tiles(local_ref):
+        before = dot(tile(spread, x, y), synth_ref[...]) + tile(local_ref, x, y)
         square = before * before
         inner = before * (GELU_SCALE + (GELU_SCALE * GELU_CUBIC) * square)
         gate = 0.5 + 0.5 * jnp.tanh(inner)
         twice = 2.0 * GELU_SCALE + (6.0 * GELU_SCALE * GELU_CUBIC) * square
         slope = 1.0 + before * (1.0 - gate) * twice
         upstream = (before * gate) * (gate * slope)
-        up_ref[:, x, pl.ds(y, ROWS)] = upstream.astype(jnp.bfloat16).reshape(channels, ROWS, cells)
-        return carry
-
-    lax.fori_loop(0, planes * (rows // ROWS), step, 0)
-    analyze(up_ref, depth_ref, row_ref, upper_ref, lower_ref, out_ref)
-
-
-def final_kernel(values_ref, grid_ref, local_ref, lift_ref, synth_ref, out_ref, spread_ref):
-    channels, planes, rows, cells = grid_ref.shape
-    lift(values_ref, lift_ref, spread_ref)
+        upstream = upstream.astype(jnp.bfloat16).reshape(channels, ROWS, cells)
+        up_ref[:, x, y : y + ROWS] = upstream
+
+    def ready(c):
+        if c == channels:
+            row_copy.wait()
+
+    analyze(up_ref, depth_ref, row_ref, upper_ref, lower_ref, kept_ref, sent_ref, ready)
+
+
+def final_kernel(
+    mine_ref, other_ref, local_ref, lift_ref, synth_ref, out_hbm, spread_ref, result_ref, out_sems
+):
+    channels, planes, rows, cells = local_ref.shape
+    lift(mine_ref, other_ref, lift_ref, spread_ref)
     spread = spread_ref.reshape(channels, planes, rows, 4 * MZ)
-
-    def step(index, carry):
-        x = index // (rows // ROWS)
-        y = pl.multiple_of((index % (rows // ROWS)) * ROWS, ROWS)
-        total = tile_sums(spread, grid_ref, synth_ref, local_ref, x, y)
-        out_ref[:, x, pl.ds(y, ROWS)] = total.astype(jnp.bfloat16).reshape(channels, ROWS, cells)
-        return carry
-
-    lax.fori_loop(0, planes * (rows // ROWS), step, 0)
+    copies = []
+    for x, y in tiles(local_ref):
+        total = dot(tile(spread, x, y), synth_ref[...]) + tile(local_ref, x, y)
+        total = total.astype(jnp.bfloat16).reshape(channels, ROWS, cells)
+        result_ref[:, x, y : y + ROWS] = total
+        copies.append(
+            fetch(
+                result_ref.at[:, x, pl.ds(y, ROWS)],
+                out_hbm.at[:, x, pl.ds(y, ROWS)],
+                out_sems.at[len(copies)],
+            )
+        )
+    for copy in copies:
+        copy.wait()
 
 
 VMEM = pl.BlockSpec(memory_space=pltpu.VMEM)
-
-
-def call(kernel, outs, scratch, *operands, flops=1 << 30, size=4 << 20):
+HBM = pl.BlockSpec(memory_space=pltpu.HBM)
+
+
+def call(kernel, outs, scratch, *operands, far=(), out_specs=None, limit=20480):
     return pl.pallas_call(
         kernel,
         out_shape=outs,
-        in_specs=[VMEM] * len(operands),
-        out_specs=jax.tree.map(lambda _: VMEM, outs),
+        in_specs=[HBM if i in far else VMEM for i in range(len(operands))],
+        out_specs=jax.tree.map(lambda _: VMEM, outs) if out_specs is None else out_specs,
         scratch_shapes=scratch,
-        compiler_params=pltpu.CompilerParams(vmem_limit_bytes=40 << 20),
-        cost_estimate=pl.CostEstimate(flops=flops, bytes_accessed=size, transcendentals=0),
+        compiler_params=pltpu.CompilerParams(vmem_limit_bytes=limit << 10),
+        cost_estimate=pl.CostEstimate(flops=1 << 30, bytes_accessed=4 << 20, transcendentals=0),
     )(*operands)
 
 
@@ -378,65 +438,90 @@
     gn = pairs // kyn
     blocks = KY // kyn
     turns = groups // gn
-    lanes = channels * groups
+    half = channels // 2
     line = kyn * 2 * planes
     modes = spectral_weight.shape[3]
 
-    row_ahead = lax.dynamic_index_in_dim(jnp.asarray(row_analysis(pencils, planes)), member, 0, False)
+    row_ahead = jnp.asarray(row_analysis(pencils, planes))
     row_back = lax.dynamic_index_in_dim(jnp.asarray(row_synthesis(pencils, planes)), member, 0, False)
     plane_ahead = jnp.asarray(plane_analysis(slabs, planes, kyn, scale))
     plane_back = jnp.asarray(plane_synthesis(slabs, planes, kyn, scale))
     swap = jnp.asarray(channel_swap(channels, gn))
     repeat = jnp.asarray(np.repeat(np.eye(channels), ROWS, axis=0).astype(BF16))
     mask = jnp.asarray(np.tile(np.eye(ROWS), (channels, channels)).astype(BF16))
+    neighbours = [(i, i ^ 1) for i in range(pencils)]
 
     def widen(weight):
         rows_wide = dot(repeat, weight).astype(jnp.bfloat16)
         return dot(rows_wide, repeat, 1, 1).astype(jnp.bfloat16) * mask
 
-    def to_owner(parts):
+    def to_owner(kept, sent, beside):
+        given = lax.ppermute(sent, "yz", neighbours)
+        given, beside = lax.optimization_barrier((given, beside))
+        parts = kept + given
         if turns > 1:
-            parts = parts.reshape(blocks, pencils, line, channels, turns, gn)
+            parts = parts.reshape(blocks, pencils, line, half, turns, gn)
             parts = jnp.transpose(parts, (0, 4, 1, 2, 3, 5))
-        parts = parts.reshape(slabs * pencils, line, channels * gn)
+        parts = parts.reshape(slabs * pencils, line, half * gn)
         moved = lax.all_to_all(parts, ("slab", "yz"), 0, 0, tiled=True)
-        return moved.reshape(slabs, pencils, line, channels * gn)
-
-    def from_owner(values):
-        values = values.reshape(slabs * pencils, line, channels * gn)
+        return moved.reshape(slabs, pencils, line, half * gn), beside
+
+    def from_owner(values, work):
+        values = values.reshape(slabs * pencils, line, half * gn)
         moved = lax.all_to_all(values, ("slab", "yz"), 0, 0, tiled=True)
         if turns > 1:
-            moved = moved.reshape(blocks, turns, pencils, line, channels, gn)
+            moved = moved.reshape(blocks, turns, pencils, line, half, gn)
             moved = jnp.transpose(moved, (0, 2, 3, 4, 1, 5))
-        return moved.reshape(blocks, pencils, line, lanes)
-
-    halves_scratch = [pltpu.VMEM((pencils, lanes, 2 * planes * rows), jnp.bfloat16)] * 2
+        moved = moved.reshape(blocks, pencils, line, half * groups)
+        other = lax.ppermute(moved, "yz", neighbours)
+        if work is None:
+            return moved, other, None
+        return lax.optimization_barrier((moved, other, work(moved)))
+
+    halves_scratch = [pltpu.VMEM((pencils, channels * groups, 2 * planes * rows), jnp.bfloat16)] * 2
+    row_scratch = pltpu.VMEM(row_ahead.shape[1:], jnp.bfloat16)
     spread_scratch = pltpu.VMEM((channels * planes * rows, 4 * MZ), jnp.bfloat16)
-    sent = f32(blocks, pencils, line, lanes)
-    given = f32(slabs, pencils, line, channels * gn)
+    field_scratch = pltpu.VMEM(grid_field.shape, jnp.bfloat16)
+    sums = f32(blocks, pencils, line, half * groups)
+    given = f32(slabs, pencils, line, half * gn)
     coefs = f32(2, channels, modes)
-
-    parts = call(
-        analyze_kernel, sent, halves_scratch,
-        grid_field, jnp.asarray(depth_analysis(pencils, False)), row_ahead,
-    )
-    received = to_owner(parts)
+    depth_ahead = jnp.asarray(depth_analysis(pencils, False))
+
+    kept, sent = call(
+        analyze_kernel, (sums, sums),
+        [
+            field_scratch, pltpu.VMEM(depth_ahead.shape, jnp.bfloat16), row_scratch, *halves_scratch,
+            pltpu.SemaphoreType.DMA((PIECES,)), pltpu.SemaphoreType.DMA((2,)),
+        ],
+        grid_field, depth_ahead, row_ahead, far=(0, 1, 2), limit=LARGE + 1536,
+    )
+    received, (wide, wide_back, row_back) = to_owner(
+        kept, sent, (widen(local_weight), widen(local_weight.T), row_back)
+    )
 
     def mix(*refs):
         mix_kernel(kyn, *refs)
 
     values, coef = call(
-        mix, (given, coefs), [pltpu.VMEM((2, channels, modes), jnp.float32)],
-        received, spectral_weight, plane_ahead, plane_back, swap,
-    )
-    upstream, parts = call(
-        middle_kernel,
-        (bf16(channels, planes, rows, cells), sent),
-        [spread_scratch] + halves_scratch,
-        from_owner(values), grid_field, widen(local_weight), row_back,
+        mix, (given, coefs),
+        [pltpu.VMEM((2, channels, modes), jnp.float32)] * 2 + [pltpu.SemaphoreType.DMA],
+        received, spectral_weight, plane_ahead, plane_back, swap, out_specs=(VMEM, HBM),
+    )
+    def local_ahead(moved):
+        _, late = lax.optimization_barrier((moved, wide))
+        return call(local_kernel, f32(*grid_field.shape), [], grid_field, late)
+
+    mine, other, local = from_owner(values, local_ahead)
+    upstream, kept, sent = call(
+        middle_kernel, (bf16(*grid_field.shape), sums, sums),
+        [spread_scratch, row_scratch, *halves_scratch, pltpu.SemaphoreType.DMA],
+        mine, other, local, row_back,
         jnp.asarray(depth_synthesis(pencils, True)), jnp.asarray(depth_analysis(pencils, True)), row_ahead,
-    )
-    received = to_owner(parts)
+        far=(6,),
+    )
+    received, local = to_owner(
+        kept, sent, call(local_kernel, f32(*grid_field.shape), [], upstream, wide_back)
+    )
 
     def unmix(*refs):
         unmix_kernel(kyn, *refs)
@@ -445,11 +530,17 @@
         unmix, (given, coefs), [],
         received, spectral_weight, plane_ahead, plane_back, swap,
     )
-    grad_weight = call(outer_kernel, f32(2, channels, channels, modes), [], coef, back)
+
+    def outer(moved):
+        _, late = lax.optimization_barrier((moved, back))
+        return call(outer_kernel, f32(2, channels, channels, modes), [], coef, late)
+
+    mine, other, grad_weight = from_owner(values, outer)
     grad_field = call(
-        final_kernel, bf16(channels, planes, rows, cells), [spread_scratch],
-        from_owner(values), upstream, widen(local_weight.T), row_back,
-        jnp.asarray(depth_synthesis(pencils, False)),
+        final_kernel, bf16(*grid_field.shape),
+        [spread_scratch, field_scratch, pltpu.SemaphoreType.DMA((planes * rows // ROWS,))],
+        mine, other, local, row_back, jnp.asarray(depth_synthesis(pencils, False)),
+        out_specs=HBM,
     )
     return grad_field, grad_weight
 

time: 80.9 us -> 66.6 us (0.82)
  waiting for transfers between devices: 15.8 us -> 0.01 us
  blocking collectives: 30.4 us -> 45.1 us
  local copies, waits for them, and re-layouts: 5.84 us -> 1.81 us
  starting transfers between devices: 5.17 us -> 1.3 us
  Pallas kernels: 19.5 us -> 16.4 us
  matrix products: 2.87 us -> 0.78 us
    all_to_all x0 -> x2, blocking collectives: none -> 20.1 us  [from_owner(): moved = lax.all_to_all(values, ('slab', 'yz'), 0, 0, tiled=True)]
    all_to_all x2 -> x0, waiting for transfers between devices: 15.8 us -> none  [from_owner(): moved = lax.all_to_all(values, ('slab', 'yz'), 0, 0, tiled=True)]
    all_to_all x2, blocking collectives: 30.4 us -> 25 us  [to_owner(): moved = lax.all_to_all(parts, ('slab', 'yz'), 0, 0, tiled=True)]
    all_to_all x2 -> x0, starting transfers between devices: 5.17 us -> none  [from_owner(): moved = lax.all_to_all(values, ('slab', 'yz'), 0, 0, tiled=True)]
    unnamed x28 -> x26, local copies, waits for them, and re-layouts: 4.08 us -> 0.91 us
    pallas_call x6 -> x8, Pallas kernels: 19.5 us -> 16.4 us  [call(): pl.pallas_call(kernel, out_shape=outs, in_specs=[HBM if i in far else VME...]
    dot_general x2, matrix products: 2.87 us -> 0.78 us  [dot(): lax.dot_general(left, right, (((left_dim,), (right_dim,)), ((), ())), pre...]
    ppermute x0 -> x4, starting transfers between devices: none -> 1.3 us  [the longest x2 0.87 us: to_owner(): given = lax.ppermute(sent, 'yz', neighbours)]
  transfers between devices with their start and end apart: 2 -> 4, of which waited for: 2 -> 0; matrix products, arithmetic and copies ran while one was open for 5% -> 3% of each run, Pallas kernels for 2% -> 6%
where the time goes in v1:
time: 66.6 us; the launch traced here: 66.3 us
  blocking collectives  45.1 us (68%)
  Pallas kernels  16.4 us (25%)
  local copies, waits for them, and re-layouts  1.81 us (3%)
  starting transfers between devices  1.3 us (2%)
  between operations  0.82 us (1%)
  matrix products  0.78 us (1%)
    all_to_all x2, blocking collectives, to_owner(): moved = lax.all_to_all(parts, ('slab', 'yz'), 0, 0, tiled=True)  25 us
    all_to_all x2, blocking collectives, from_owner(): moved = lax.all_to_all(values, ('slab', 'yz'), 0, 0, tiled=True)  20.1 us
    pallas_call x8, Pallas kernels, call(): pl.pallas_call(kernel, out_shape=outs, in_specs=[HBM if i in far else VME...  16.4 us
  transfers between devices with their start and end apart: 4, of which 0 were waited for; matrix products, arithmetic and copies ran while one was open for 3% of the time, Pallas kernels for 6%

profile of v1, /device:TPU:0, one launch (start us, length us, event | category | flops | bytes accessed | tf_op | source)
XLA Modules:
  0.0 66.3 jit_solution(3032537453699043220)
XLA Ops:
  0.6 0.0 copy-start
  0.6 0.0 copy-start.9
  0.7 0.8 %copy-done.9 = bf16[128,256]{1,0:T(8,128)(2,1)S(1)} copy-done((bf16[128,256]{1,0:T(8,128)(2,1)S(1)}, bf16[128,256]{1,0:T(8,128)(2,1)}, u32[]{:S(2)}) %copy-start.9) | copy-done | bytes 65560
  1.5 2.8 %shard_map.149 = (f32[8,4,8,128]{3,2,1,0:T(8,128)S(1)}, f32[8,4,8,128]{3,2,1,0:T(8,128)S(1)}) custom-call(bf16[32,2,64,256]{3,2,1,0:T(8,128)(2,1)} %grid_ref.1, bf16[128,256]{1,0:T(8,128)(2,1)S(1)} %copy-done.9, bf16[4,128,256]{2,1,0:T(8,128)(2,1)} %constant.32.clone.row_hbm), custom_call_target="tpu_custom_call" | custom-call | flops 1073741824 | bytes 4194304 | tf_op jit(solution)/shard_map/pallas_call | solution.py:410
  4.3 0.0 copy-start.6
  4.3 0.0 copy-start.7
  4.3 0.0 copy-start.8
  4.3 0.0 copy-start.10
  4.4 0.5 collective-permute-start
  4.9 0.4 fusion.1.wide_ref
  5.3 0.4 fusion.wide_ref
  5.7 0.9 %dynamic-slice_bitcast_fusion.lift_ref = bf16[192,256]{1,0:T(8,128)(2,1)S(1)} fusion(bf16[4,192,256]{2,1,0:T(8,128)(2,1)} %constant.33.clone, s32[]{:T(128)S(6)} %select_n.4), kind=kLoop, calls=%fused_computation.6 | loop fusion | bytes 196612 | tf_op jit(solution)/shard_map/jit(dynamic_index_in_dim)/squeeze | solution.py:446
  6.6 0.0 collective-permute-done
  6.6 15.0 %all_to_all.20 = f32[32,8,128]{2,1,0:T(8,128)S(1)} all-to-all(f32[32,8,128]{2,1,0:T(8,128)S(1)} %bitcast.24), channel_id=1, replica_groups=mesh['slab'=8,'yz'=4] {'slab','yz'}, dimensions={0} | all-to-all | bytes 262144 | tf_op jit(solution)/shard_map/all_to_all | solution.py:466
  21.6 0.0 copy-start.1
  21.7 1.7 %shard_map.150 = (f32[8,4,8,128]{3,2,1,0:T(8,128)S(1)}, f32[2,32,256]{2,1,0:T(8,128)S(1)}) custom-call(f32[8,4,8,128]{3,2,1,0:T(8,128)S(1)} %bitcast.22, bf16[2,32,32,256]{3,2,1,0:T(8,128)(2,1)S(1)} %copy-done.6, bf16[2,128,64]{2,1,0:T(8,128)(2,1)S(1)} %copy-done.8, bf16[2,64,64]{2,1,0:T(8,128)(2,1)S(1)} %copy-done.10, bf16[256,256]{1,0:T(8,128)(2,1)S(1)} %copy-done.7), custom_call_target="tpu_custom_call" | custom-call | flops 1073741824 | bytes 4194304 | tf_op jit(solution)/shard_map/pallas_call | solution.py:410
  23.3 10.0 %all_to_all.21 = f32[32,8,128]{2,1,0:T(8,128)S(1)} all-to-all(f32[32,8,128]{2,1,0:T(8,128)S(1)} %bitcast.23), channel_id=1, replica_groups=mesh['slab'=8,'yz'=4] {'slab','yz'}, dimensions={0} | all-to-all | bytes 262144 | tf_op jit(solution)/shard_map/all_to_all | solution.py:471
  33.3 0.2 collective-permute-start.1
  33.5 1.3 %shard_map.151.local_ref = f32[32,2,64,256]{3,2,1,0:T(8,128)S(1)} custom-call(bf16[32,2,64,256]{3,2,1,0:T(8,128)(2,1)S(1)} %copy-done.1, bf16[512,512]{1,0:T(8,128)(2,1)S(1)} %fusion.wide_ref), custom_call_target="tpu_custom_call" | custom-call | flops 1073741824 | bytes 4194304 | tf_op jit(solution)/shard_map/pallas_call | solution.py:410
  34.8 0.0 collective-permute-done.1.other_ref
  34.8 4.2 %shard_map.152 = (bf16[32,2,64,256]{3,2,1,0:T(8,128)(2,1)S(1)}, f32[8,4,8,128]{3,2,1,0:T(8,128)S(1)}, f32[8,4,8,128]{3,2,1,0:T(8,128)S(1)}) custom-call(f32[8,4,8,128]{3,2,1,0:T(8,128)S(1)} %bitcast.17, f32[8,4,8,128]{3,2,1,0:T(8,128)S(1)} %collective-permute-done.1.other_ref, f32[32,2,64,256]{3,2,1,0:T(8,128)S(1)} %shard_map.151.local_ref, ...), custom_call_target="tpu_custom_call" | custom-call | flops 1073741824 | bytes 4194304 | tf_op jit(solution)/shard_map/pallas_call | solution.py:410
  39.0 0.4 collective-permute-start.2
  39.4 1.2 %shard_map.153.local_ref = f32[32,2,64,256]{3,2,1,0:T(8,128)S(1)} custom-call(bf16[32,2,64,256]{3,2,1,0:T(8,128)(2,1)S(1)} %get-tuple-element.37.grid_ref, bf16[512,512]{1,0:T(8,128)(2,1)S(1)} %fusion.1.wide_ref), custom_call_target="tpu_custom_call" | custom-call | flops 1073741824 | bytes 4194304 | tf_op jit(solution)/shard_map/pallas_call | solution.py:410
  40.7 0.0 collective-permute-done.2
  40.7 10.0 %all_to_all.22 = f32[32,8,128]{2,1,0:T(8,128)S(1)} all-to-all(f32[32,8,128]{2,1,0:T(8,128)S(1)} %bitcast.25), channel_id=1, replica_groups=mesh['slab'=8,'yz'=4] {'slab','yz'}, dimensions={0} | all-to-all | bytes 262144 | tf_op jit(solution)/shard_map/all_to_all | solution.py:466
  50.7 1.5 %shard_map.154 = (f32[8,4,8,128]{3,2,1,0:T(8,128)S(1)}, f32[2,32,256]{2,1,0:T(8,128)S(1)}) custom-call(f32[8,4,8,128]{3,2,1,0:T(8,128)S(1)} %bitcast.20, bf16[2,32,32,256]{3,2,1,0:T(8,128)(2,1)S(1)} %copy-done.6, bf16[2,128,64]{2,1,0:T(8,128)(2,1)S(1)} %copy-done.8, bf16[2,64,64]{2,1,0:T(8,128)(2,1)S(1)} %copy-done.10, bf16[256,256]{1,0:T(8,128)(2,1)S(1)} %copy-done.7), custom_call_target="tpu_custom_call" | custom-call | flops 1073741824 | bytes 4194304 | tf_op jit(solution)/shard_map/pallas_call | solution.py:410
  52.2 0.0 copy-start.3
  52.2 10.1 %all_to_all.23 = f32[32,8,128]{2,1,0:T(8,128)S(1)} all-to-all(f32[32,8,128]{2,1,0:T(8,128)S(1)} %bitcast.21), channel_id=1, replica_groups=mesh['slab'=8,'yz'=4] {'slab','yz'}, dimensions={0} | all-to-all | bytes 262144 | tf_op jit(solution)/shard_map/all_to_all | solution.py:471
  62.3 0.2 collective-permute-start.3
  62.5 1.5 %shard_map.155 = f32[2,32,32,256]{3,2,1,0:T(8,128)} custom-call(f32[2,32,256]{2,1,0:T(8,128)S(1)} %get-tuple-element.41.coef_ref, f32[2,32,256]{2,1,0:T(8,128)S(1)} %get-tuple-element.43.back_ref), custom_call_target="tpu_custom_call" | custom-call | flops 1073741824 | bytes 4194304 | tf_op jit(solution)/shard_map/pallas_call | solution.py:410
  64.1 0.0 collective-permute-done.3.other_ref
  64.1 2.2 %shard_map.156 = bf16[32,2,64,256]{3,2,1,0:T(8,128)(2,1)} custom-call(f32[8,4,8,128]{3,2,1,0:T(8,128)S(1)} %bitcast.19, f32[8,4,8,128]{3,2,1,0:T(8,128)S(1)} %collective-permute-done.3.other_ref, f32[32,2,64,256]{3,2,1,0:T(8,128)S(1)} %shard_map.153.local_ref, bf16[192,256]{1,0:T(8,128)(2,1)S(1)} %dynamic-slice_bitcast_fusion.lift_ref, ...), custom_call_target="tpu_custom_call" | custom-call | flops 1073741824 | bytes 4194304 | tf_op jit(solution)/shard_map/pallas_call | solution.py:410
  (19 shorter events, 0.1 us)
Async XLA Ops:
  0.6 4.2 %copy-start = (bf16[32,32]{1,0:T(8,128)(2,1)S(1)}, bf16[32,32]{1,0:T(8,128)(2,1)}, u32[]{:S(2)}) copy-start(bf16[32,32]{1,0:T(8,128)(2,1)} %param.16) | copy-start | bytes 6148
  0.6 0.8 %copy-start.9 = (bf16[128,256]{1,0:T(8,128)(2,1)S(1)}, bf16[128,256]{1,0:T(8,128)(2,1)}, u32[]{:S(2)}) copy-start(bf16[128,256]{1,0:T(8,128)(2,1)} %constant.39.clone.depth_hbm) | copy-start | bytes 196612
  1.5 3.4 %copy-start.11 = (bf16[512,32]{1,0:T(8,128)(2,1)S(1)}, bf16[512,32]{1,0:T(8,128)(2,1)}, u32[]{:S(2)}) copy-start(bf16[512,32]{1,0:T(8,128)(2,1)} %constant.37.clone) | copy-start | bytes 98308
  1.5 3.4 %copy-start.12 = (bf16[512,512]{1,0:T(8,128)(2,1)S(1)}, bf16[512,512]{1,0:T(8,128)(2,1)}, u32[]{:S(2)}) copy-start(bf16[512,512]{1,0:T(8,128)(2,1)} %constant.38.clone) | copy-start | bytes 1572868
  4.3 17.3 %copy-start.6 = (bf16[2,32,32,256]{3,2,1,0:T(8,128)(2,1)S(1)}, bf16[2,32,32,256]{3,2,1,0:T(8,128)(2,1)}, u32[]{:S(2)}) copy-start(bf16[2,32,32,256]{3,2,1,0:T(8,128)(2,1)} %refs_1_.3) | copy-start | bytes 3145732
  4.3 17.3 %copy-start.7 = (bf16[256,256]{1,0:T(8,128)(2,1)S(1)}, bf16[256,256]{1,0:T(8,128)(2,1)}, u32[]{:S(2)}) copy-start(bf16[256,256]{1,0:T(8,128)(2,1)} %constant.36.clone.refs_4_) | copy-start | bytes 393220
  4.3 17.3 %copy-start.8 = (bf16[2,128,64]{2,1,0:T(8,128)(2,1)S(1)}, bf16[2,128,64]{2,1,0:T(8,128)(2,1)}, u32[]{:S(2)}) copy-start(bf16[2,128,64]{2,1,0:T(8,128)(2,1)} %constant.34.clone.refs_2_) | copy-start | bytes 98308
  4.3 17.3 %copy-start.10 = (bf16[2,64,64]{2,1,0:T(8,128)(2,1)S(1)}, bf16[2,64,64]{2,1,0:T(8,128)(2,1)}, u32[]{:S(2)}) copy-start(bf16[2,64,64]{2,1,0:T(8,128)(2,1)} %constant.35.clone.refs_3_) | copy-start | bytes 49156
  4.4 2.2 %collective-permute-start = (f32[8,4,8,128]{3,2,1,0:T(8,128)S(1)}, f32[8,4,8,128]{3,2,1,0:T(8,128)S(1)}, u32[]{:S(2)}, u32[]{:S(2)}) collective-permute-start(f32[8,4,8,128]{3,2,1,0:T(8,128)S(1)} %get-tuple-element.26), channel_id=1, source_target_pairs={{0,1},{1,0},{2,3},{3,2},{4,5},{5,4},{6,7},{7,6},{8,9},{9,8},{10,11... | collective-permute-start | bytes 393224 | tf_op jit(solution)/shard_map/ppermute | solution.py:459
  21.6 11.9 %copy-start.1 = (bf16[32,2,64,256]{3,2,1,0:T(8,128)(2,1)S(1)}, bf16[32,2,64,256]{3,2,1,0:T(8,128)(2,1)}, u32[]{:S(2)}) copy-start(bf16[32,2,64,256]{3,2,1,0:T(8,128)(2,1)} %grid_ref.1) | copy-start | bytes 6291460
  33.3 1.5 %copy-start.2 = (bf16[4,128,256]{2,1,0:T(8,128)(2,1)S(1)}, bf16[4,128,256]{2,1,0:T(8,128)(2,1)}, u32[]{:S(2)}) copy-start(bf16[4,128,256]{2,1,0:T(8,128)(2,1)} %constant.32.clone.row_hbm) | copy-start | bytes 786436
  33.3 1.5 %copy-start.4 = (bf16[128,256]{1,0:T(8,128)(2,1)S(1)}, bf16[128,256]{1,0:T(8,128)(2,1)}, u32[]{:S(2)}) copy-start(bf16[128,256]{1,0:T(8,128)(2,1)} %constant.41.clone.depth_ref) | copy-start | bytes 196612
  33.3 1.5 %copy-start.5 = (bf16[128,256]{1,0:T(8,128)(2,1)S(1)}, bf16[128,256]{1,0:T(8,128)(2,1)}, u32[]{:S(2)}) copy-start(bf16[128,256]{1,0:T(8,128)(2,1)} %constant.40.clone.synth_ref) | copy-start | bytes 196612
  33.3 1.5 %collective-permute-start.1 = (f32[8,4,8,128]{3,2,1,0:T(8,128)S(1)}, f32[8,4,8,128]{3,2,1,0:T(8,128)S(1)}, u32[]{:S(2)}, u32[]{:S(2)}) collective-permute-start(f32[8,4,8,128]{3,2,1,0:T(8,128)S(1)} %bitcast.16), channel_id=1, source_target_pairs={{0,1},{1,0},{2,3},{3,2},{4,5},{5,4},{6,7},{7,6},{8,9},{9,8},{10,11... | collective-permute-start | bytes 393224 | tf_op jit(solution)/shard_map/ppermute | solution.py:476
  39.0 1.6 %collective-permute-start.2 = (f32[8,4,8,128]{3,2,1,0:T(8,128)S(1)}, f32[8,4,8,128]{3,2,1,0:T(8,128)S(1)}, u32[]{:S(2)}, u32[]{:S(2)}) collective-permute-start(f32[8,4,8,128]{3,2,1,0:T(8,128)S(1)} %get-tuple-element.36), channel_id=1, source_target_pairs={{0,1},{1,0},{2,3},{3,2},{4,5},{5,4},{6,7},{7,6},{8,9},{9,8},{10,11... | collective-permute-start | bytes 393224 | tf_op jit(solution)/shard_map/ppermute | solution.py:459
  52.2 11.8 %copy-start.3 = (bf16[128,256]{1,0:T(8,128)(2,1)S(1)}, bf16[128,256]{1,0:T(8,128)(2,1)}, u32[]{:S(2)}) copy-start(bf16[128,256]{1,0:T(8,128)(2,1)} %constant.42.clone.synth_ref) | copy-start | bytes 196612
  62.3 1.8 %collective-permute-start.3 = (f32[8,4,8,128]{3,2,1,0:T(8,128)S(1)}, f32[8,4,8,128]{3,2,1,0:T(8,128)S(1)}, u32[]{:S(2)}, u32[]{:S(2)}) collective-permute-start(f32[8,4,8,128]{3,2,1,0:T(8,128)S(1)} %bitcast.18), channel_id=1, source_target_pairs={{0,1},{1,0},{2,3},{3,2},{4,5},{5,4},{6,7},{7,6},{8,9},{9,8},{10,11... | collective-permute-start | bytes 393224 | tf_op jit(solution)/shard_map/ppermute | solution.py:476

commit v2 on v1

v2 whole, which is shorter than its diff:
```python
import math

import jax
import jax.numpy as jnp
import ml_dtypes
import numpy as np
from jax import lax
from jax.experimental import pallas as pl
from jax.experimental.pallas import tpu as pltpu
from jax.sharding import PartitionSpec as P

KX = 16
KY = 16
MZ = 32
NY = 256
NZ = 256
ROWS = 8
LANES = 128
PIECES = 2
OUTER = 4

GELU_SCALE = 0.7978845608028654
GELU_CUBIC = 0.044715
BF16 = ml_dtypes.bfloat16
LARGE = 54272


def freqs(number, length):
    index = np.arange(number)
    return np.where(index < number // 2, index, length - number + index)


def angles(positions, frequencies, length):
    phase = (positions[:, None].astype(np.int64) * frequencies[None, :]) % length
    return phase * (2.0 * math.pi / length)


def halves(matrix):
    matrix = np.asarray(matrix, np.float32)
    upper = matrix.astype(BF16)
    lower = (matrix - upper.astype(np.float32)).astype(BF16)
    return upper, lower


def depth_freqs(pencils):
    groups = MZ // pencils
    return np.array([[g * pencils + q for g in range(groups)] for q in range(pencils)])


def depth_analysis(pencils, doubled):
    kz = depth_freqs(pencils)
    theta = angles(kz.reshape(-1), np.arange(NZ), NZ).reshape(pencils, -1, NZ)
    weight = np.where(kz == 0, 1.0, 2.0 if doubled else 1.0)[:, :, None]
    table = np.stack([np.cos(theta) * weight, -np.sin(theta) * weight], axis=1)
    return np.concatenate(halves(table.reshape(2 * MZ, NZ)), axis=0)


def depth_synthesis(pencils, doubled):
    kz = depth_freqs(pencils)
    theta = angles(kz.reshape(-1), np.arange(NZ), NZ).reshape(pencils, -1, NZ)
    weight = np.where(kz == 0, 1.0, 2.0 if doubled else 1.0)[:, :, None]
    table = np.stack([np.cos(theta) * weight, -np.sin(theta) * weight], axis=1)
    return np.tile(table.reshape(2 * MZ, NZ), (2, 1)).astype(BF16)


def row_analysis(pencils, planes):
    rows = NY // pencils
    tables = []
    for member in range(pencils):
        theta = angles(freqs(KY, NY), member * rows + np.arange(rows), NY)
        table = np.zeros((KY, 2, planes, 2, planes, rows))
        for x in range(planes):
            table[:, 0, x, 0, x] = np.cos(theta)
            table[:, 0, x, 1, x] = np.sin(theta)
            table[:, 1, x, 0, x] = -np.sin(theta)
            table[:, 1, x, 1, x] = np.cos(theta)
        table = table.reshape(KY * 2 * planes, 2 * planes * rows)
        tables.append(np.concatenate(halves(table), axis=0))
    return np.stack(tables)


def row_synthesis(pencils, planes):
    rows = NY // pencils
    tables = []
    for member in range(pencils):
        theta = angles(freqs(KY, NY), member * rows + np.arange(rows), NY)
        table = np.zeros((KY, 2, planes, 2, planes, rows))
        for x in range(planes):
            table[:, 0, x, 0, x] = np.cos(theta)
            table[:, 1, x, 0, x] = -np.sin(theta)
            table[:, 0, x, 1, x] = np.sin(theta)
            table[:, 1, x, 1, x] = np.cos(theta)
        upper, lower = halves(table.reshape(KY * 2 * planes, 2 * planes * rows))
        tables.append(np.concatenate([upper, upper, lower], axis=0))
    return np.stack(tables)


def member_tables(pencils, planes):
    depth = depth_analysis(pencils, False)
    ahead = row_analysis(pencils, planes)
    back = row_synthesis(pencils, planes)
    return np.stack([np.concatenate([depth, ahead[q], back[q]], 0) for q in range(pencils)])


def padded(table):
    return np.pad(table, ((0, 0), (0, max(0, LANES - table.shape[1]))))


def plane_analysis(slabs, planes, kyn, scale):
    theta = angles(np.arange(slabs * planes), freqs(KX, slabs * planes), slabs * planes)
    theta = theta.reshape(slabs, planes, KX)
    table = np.zeros((slabs, kyn, 2, planes, 2, kyn, KX))
    for k in range(kyn):
        table[:, k, 0, :, 0, k] = np.cos(theta)
        table[:, k, 1, :, 0, k] = np.sin(theta)
        table[:, k, 0, :, 1, k] = -np.sin(theta)
        table[:, k, 1, :, 1, k] = np.cos(theta)
    table = scale * table.reshape(slabs * kyn * 2 * planes, 2 * kyn * KX)
    upper, lower = halves(padded(table))
    return np.concatenate([upper, upper, lower], axis=0)


def plane_synthesis(slabs, planes, kyn, scale):
    theta = angles(np.arange(slabs * planes), freqs(KX, slabs * planes), slabs * planes)
    theta = theta.reshape(slabs, planes, KX)
    table = np.zeros((slabs, kyn, 2, planes, 2, kyn, KX))
    for k in range(kyn):
        table[:, k, 0, :, 0, k] = np.cos(theta)
        table[:, k, 0, :, 1, k] = -np.sin(theta)
        table[:, k, 1, :, 0, k] = np.sin(theta)
        table[:, k, 1, :, 1, k] = np.cos(theta)
    table = scale * table.reshape(slabs * kyn * 2 * planes, 2 * kyn * KX)
    return np.stack(halves(padded(table)))


def split(value):
    upper = value.astype(jnp.bfloat16)
    return upper, (value - upper.astype(jnp.float32)).astype(jnp.bfloat16)


def dot(left, right, left_dim=1, right_dim=0):
    return lax.dot_general(
        left, right, (((left_dim,), (right_dim,)), ((), ())), preferred_element_type=jnp.float32
    )


def analyze_depth(c, block, depth_ref, upper_ref, lower_ref):
    pencils, _, width = upper_ref.shape
    width = width // 2
    groups = MZ // pencils
    depth = dot(depth_ref[...], block, 1, 1)
    depth = depth[: 2 * MZ] + depth[2 * MZ :]
    for q in range(pencils):
        base = q * 2 * groups
        lines = [
            jnp.concatenate(
                [
                    depth[base : base + groups, e * width : (e + 1) * width],
                    depth[base + groups : base + 2 * groups, e * width : (e + 1) * width],
                ],
                axis=1,
            )
            for e in range(2)
        ]
        upper, lower = split(jnp.concatenate(lines, axis=0))
        upper_ref[q, c * groups : (c + 2) * groups] = upper
        lower_ref[q, c * groups : (c + 2) * groups] = lower


def analyze_rows(row_ref, upper_ref, lower_ref, kept_ref, sent_ref):
    blocks, pencils, line, half = kept_ref.shape
    count = row_ref.shape[0] // 2
    first = lax.axis_index("yz") % 2 == 0
    for q in range(pencils):
        both = dot(row_ref[...], upper_ref[q], 1, 1)
        total = both[:count] + both[count:] + dot(row_ref[:count], lower_ref[q], 1, 1)
        low = total[:, :half].reshape(blocks, line, half)
        high = total[:, half:].reshape(blocks, line, half)
        kept_ref[:, q] = jnp.where(first, low, high)
        sent_ref[:, q] = jnp.where(first, high, low)


def fetch(hbm, ref, sem):
    copy = pltpu.make_async_copy(hbm, ref, sem)
    copy.start()
    return copy


def analyze_kernel(
    grid_hbm, table_hbm, kept_ref, sent_ref, row_ref, lift_ref,
    grid_ref, depth_ref, upper_ref, lower_ref, piece_sem, table_sem,
):
    channels, planes, rows, cells = grid_hbm.shape
    step = channels // PIECES
    table = table_hbm.at[lax.axis_index("yz")]
    first = depth_ref.shape[0]
    second = first + row_ref.shape[0]
    depth_copy = fetch(table.at[pl.ds(0, first)], depth_ref, table_sem.at[0])
    pieces = [
        fetch(grid_hbm.at[pl.ds(i * step, step)], grid_ref.at[pl.ds(i * step, step)], piece_sem.at[i])
        for i in range(PIECES)
    ]
    row_copy = fetch(table.at[pl.ds(first, row_ref.shape[0])], row_ref, table_sem.at[1])
    lift_copy = fetch(table.at[pl.ds(second, lift_ref.shape[0])], lift_ref, table_sem.at[2])
    depth_copy.wait()
    for c in range(0, channels, 2):
        if c % step == 0:
            pieces[c // step].wait()
        block = grid_ref[c : c + 2].reshape(2 * planes * rows, cells)
        analyze_depth(c, block, depth_ref, upper_ref, lower_ref)
    row_copy.wait()
    analyze_rows(row_ref, upper_ref, lower_ref, kept_ref, sent_ref)
    lift_copy.wait()


def collect(sums_ref, plane_ref, turn_ref, kyn, channels):
    slabs, pencils, line, half = sums_ref.shape
    sides = []
    for core in range(2):
        side = sums_ref[:, core]
        for member in range(core + 2, pencils, 2):
            side = side + sums_ref[:, member]
        sides.append(side.reshape(slabs * line, half))
    upper, lower = split(jnp.concatenate(sides, axis=1))
    turn_ref[...] = dot(jnp.concatenate([upper, lower, upper], axis=0), plane_ref[...], 0, 0)
    groups = 2 * half // channels
    lines = [turn_ref[pl.ds(g, channels, stride=groups)] for g in range(groups)]
    parts = []
    for part in range(2):
        pieces = []
        for k in range(kyn):
            start = (part * kyn + k) * KX
            pieces += [line[:, start : start + KX] for line in lines]
        parts.append(jnp.concatenate(pieces, axis=1) if len(pieces) > 1 else pieces[0])
    return parts


def distribute(real, imag, plane_ref, turn_ref, kyn, out_ref):
    slabs, pencils, line, half = out_ref.shape
    channels = real.shape[0]
    groups = 2 * half // channels
    for g in range(groups):
        pieces = []
        for value in (real, imag):
            for k in range(kyn):
                start = (k * groups + g) * KX
                pieces.append(value[:, start : start + KX])
        rest = turn_ref.shape[1] - 2 * kyn * KX
        if rest:
            pieces.append(jnp.zeros((channels, rest), jnp.float32))
        turn_ref[pl.ds(g, channels, stride=groups)] = jnp.concatenate(pieces, axis=1)
    upper, lower = split(turn_ref[...])
    total = (
        dot(plane_ref[0], upper, 1, 1)
        + dot(plane_ref[1], upper, 1, 1)
        + dot(plane_ref[0], lower, 1, 1)
    )
    for member in range(pencils):
        side = total[:, member % 2 * half : (member % 2 + 1) * half]
        out_ref[:, member] = side.reshape(slabs, line, half)


def mix_kernel(
    kyn, sums_ref, weight_ref, ahead_ref, back_ref, out_ref, coef_hbm, coef_ref, mixed_ref, turn_ref, sem
):
    real, imag = collect(sums_ref, ahead_ref, turn_ref, kyn, weight_ref.shape[1])
    coef_ref[0] = real
    coef_ref[1] = imag
    copy = fetch(coef_ref, coef_hbm, sem)
    for o in range(weight_ref.shape[1]):
        weight_real = weight_ref[0, o].astype(jnp.float32)
        weight_imag = weight_ref[1, o].astype(jnp.float32)
        mixed_ref[0, o : o + 1] = jnp.sum(
            weight_real * real - weight_imag * imag, axis=0, keepdims=True
        )
        mixed_ref[1, o : o + 1] = jnp.sum(
            weight_real * imag + weight_imag * real, axis=0, keepdims=True
        )
    distribute(mixed_ref[0], mixed_ref[1], back_ref, turn_ref, kyn, out_ref)
    copy.wait()


def unmix_kernel(kyn, sums_ref, weight_ref, ahead_ref, back_ref, out_ref, coef_ref, turn_ref):
    real, imag = collect(sums_ref, ahead_ref, turn_ref, kyn, weight_ref.shape[1])
    coef_ref[0] = real
    coef_ref[1] = imag
    modes_real = jnp.zeros_like(real)
    modes_imag = jnp.zeros_like(real)
    for o in range(weight_ref.shape[1]):
        weight_real = weight_ref[0, o].astype(jnp.float32)
        weight_imag = weight_ref[1, o].astype(jnp.float32)
        back_real = coef_ref[0, o : o + 1]
        back_imag = coef_ref[1, o : o + 1]
        modes_real = modes_real + (weight_real * back_real + weight_imag * back_imag)
        modes_imag = modes_imag + (weight_real * back_imag - weight_imag * back_real)
    distribute(modes_real, modes_imag, back_ref, turn_ref, kyn, out_ref)


def outer_kernel(coef_ref, back_ref, out_hbm, out_ref, sems):
    real, imag = coef_ref[0], coef_ref[1]
    channels = back_ref.shape[1]
    step = channels // OUTER
    copies = []
    for o in range(channels):
        back_real = back_ref[0, o : o + 1]
        back_imag = back_ref[1, o : o + 1]
        out_ref[0, o] = back_real * real + back_imag * imag
        out_ref[1, o] = back_imag * real - back_real * imag
        if (o + 1) % step == 0:
            start = o + 1 - step
            for part in range(2):
                copies.append(
                    fetch(
                        out_ref.at[part, pl.ds(start, step)],
                        out_hbm.at[part, pl.ds(start, step)],
                        sems.at[len(copies)],
                    )
                )
    for copy in copies:
        copy.wait()


def lift(mine_ref, other_ref, row_ref):
    blocks, pencils, line, half = mine_ref.shape
    first = lax.axis_index("yz") % 2 == 0
    lines = []
    for q in range(pencils):
        mine = mine_ref[:, q].reshape(blocks * line, half)
        other = other_ref[:, q].reshape(blocks * line, half)
        value = jnp.concatenate(
            [jnp.where(first, mine, other), jnp.where(first, other, mine)], axis=1
        )
        upper, lower = split(value)
        stacked = jnp.concatenate([upper, lower, upper], axis=0)
        lines.append(dot(stacked, row_ref[...], 0, 0))
    return lines


def spread(lines, o):
    groups = MZ // len(lines)
    lanes = lines[0].shape[1] // 2
    block = jnp.concatenate(
        [
            line[o * groups : (o + 1) * groups, part * lanes : (part + 1) * lanes]
            for line in lines
            for part in range(2)
        ],
        axis=0,
    )
    upper = block.astype(jnp.bfloat16).astype(jnp.float32)
    return jnp.concatenate([upper, block - upper], axis=0).T.astype(jnp.bfloat16)


def local_kernel(grid_ref, wide_ref, out_ref):
    channels, planes, rows, cells = grid_ref.shape
    for x in range(planes):
        for y in range(0, rows, 2 * ROWS):
            block = grid_ref[:, x, y : y + 2 * ROWS]
            for start in (0, ROWS):
                part = block[:, start : start + ROWS].reshape(channels * ROWS, cells)
                total = dot(wide_ref[...], part).reshape(channels, ROWS, cells)
                out_ref[:, x, y + start : y + start + ROWS] = total


def middle_kernel(
    mine_ref, other_ref, local_ref, lift_ref, synth_ref, depth_ref, row_ref,
    up_ref, kept_ref, sent_ref, upper_ref, lower_ref,
):
    channels, planes, rows, cells = local_ref.shape
    lines = lift(mine_ref, other_ref, lift_ref)
    for o in range(0, channels, 2):
        blocks = []
        for e in range(o, o + 2):
            before = dot(spread(lines, e), synth_ref[...])
            before = before + local_ref[e].reshape(planes * rows, cells)
            square = before * before
            tangent = jnp.tanh(before * (GELU_SCALE + (GELU_SCALE * GELU_CUBIC) * square))
            above = 1.0 + tangent
            below = 1.0 - tangent
            quarter = 0.25 * GELU_SCALE + (0.75 * GELU_SCALE * GELU_CUBIC) * square
            upstream = (before * (above * above)) * (0.25 + (before * below) * quarter)
            blocks.append(upstream.astype(jnp.bfloat16))
            up_ref[e] = blocks[-1].reshape(planes, rows, cells)
        analyze_depth(o, jnp.concatenate(blocks, axis=0), depth_ref, upper_ref, lower_ref)
    analyze_rows(row_ref, upper_ref, lower_ref, kept_ref, sent_ref)


def final_kernel(
    mine_ref, other_ref, local_ref, lift_ref, synth_ref, out_hbm, result_ref, out_sems
):
    channels, planes, rows, cells = local_ref.shape
    lines = lift(mine_ref, other_ref, lift_ref)
    step = channels // OUTER
    copies = []
    for o in range(channels):
        total = dot(spread(lines, o), synth_ref[...])
        total = total + local_ref[o].reshape(planes * rows, cells)
        result_ref[o] = total.astype(jnp.bfloat16).reshape(planes, rows, cells)
        if (o + 1) % step == 0:
            part = pl.ds(o + 1 - step, step)
            copies.append(fetch(result_ref.at[part], out_hbm.at[part], out_sems.at[len(copies)]))
    for copy in copies:
        copy.wait()


VMEM = pl.BlockSpec(memory_space=pltpu.VMEM)
HBM = pl.BlockSpec(memory_space=pltpu.HBM)


def call(kernel, outs, scratch, *operands, far=(), out_specs=None, limit=20480):
    return pl.pallas_call(
        kernel,
        out_shape=outs,
        in_specs=[HBM if i in far else VMEM for i in range(len(operands))],
        out_specs=jax.tree.map(lambda _: VMEM, outs) if out_specs is None else out_specs,
        scratch_shapes=scratch,
        compiler_params=pltpu.CompilerParams(vmem_limit_bytes=limit << 10),
        cost_estimate=pl.CostEstimate(flops=1 << 30, bytes_accessed=4 << 20, transcendentals=0),
    )(*operands)


def f32(*shape):
    return jax.ShapeDtypeStruct(shape, jnp.float32)


def bf16(*shape):
    return jax.ShapeDtypeStruct(shape, jnp.bfloat16)


def on_device(grid_field, spectral_weight, local_weight):
    channels, planes, rows, cells = grid_field.shape
    slabs = lax.axis_size("slab")
    pencils = lax.axis_size("yz")
    groups = MZ // pencils
    scale = 1.0 / math.sqrt(planes * slabs * NY * NZ)
    pairs = KY * groups // slabs
    kyn = max(1, pairs // groups)
    gn = pairs // kyn
    blocks = KY // kyn
    turns = groups // gn
    half = channels // 2
    line = kyn * 2 * planes
    modes = spectral_weight.shape[3]

    table = jnp.asarray(member_tables(pencils, planes))
    plane_ahead = jnp.asarray(plane_analysis(slabs, planes, kyn, scale))
    plane_back = jnp.asarray(plane_synthesis(slabs, planes, kyn, scale))
    repeat = jnp.asarray(np.repeat(np.eye(channels), ROWS, axis=0).astype(BF16))
    mask = jnp.asarray(np.tile(np.eye(ROWS), (channels, channels)).astype(BF16))
    neighbours = [(i, i ^ 1) for i in range(pencils)]

    def widen(weight):
        rows_wide = dot(repeat, weight).astype(jnp.bfloat16)
        return dot(rows_wide, repeat, 1, 1).astype(jnp.bfloat16) * mask

    def to_owner(kept, sent, beside):
        given = lax.ppermute(sent, "yz", neighbours)
        given, beside = lax.optimization_barrier((given, beside))
        parts = kept + given
        if turns > 1:
            parts = parts.reshape(blocks, pencils, line, half, turns, gn)
            parts = jnp.transpose(parts, (0, 4, 1, 2, 3, 5))
        parts = parts.reshape(slabs * pencils, line, half * gn)
        moved = lax.all_to_all(parts, ("slab", "yz"), 0, 0, tiled=True)
        return moved.reshape(slabs, pencils, line, half * gn), beside

    def from_owner(values, work):
        values = values.reshape(slabs * pencils, line, half * gn)
        moved = lax.all_to_all(values, ("slab", "yz"), 0, 0, tiled=True)
        if turns > 1:
            moved = moved.reshape(blocks, turns, pencils, line, half, gn)
            moved = jnp.transpose(moved, (0, 2, 3, 4, 1, 5))
        moved = moved.reshape(blocks, pencils, line, half * groups)
        other = lax.ppermute(moved, "yz", neighbours)
        if work is None:
            return moved, other, None
        return lax.optimization_barrier((moved, other, work(moved)))

    halves_scratch = [pltpu.VMEM((pencils, channels * groups, 2 * planes * rows), jnp.bfloat16)] * 2
    turn_scratch = pltpu.VMEM((channels * gn, plane_ahead.shape[1]), jnp.float32)
    field_scratch = pltpu.VMEM(grid_field.shape, jnp.bfloat16)
    sums = f32(blocks, pencils, line, half * groups)
    given = f32(slabs, pencils, line, half * gn)
    coefs = f32(2, channels, modes)
    values_count = KY * 2 * planes

    kept, sent, row_ahead, row_back = call(
        analyze_kernel, (sums, sums, bf16(2 * values_count, 2 * planes * rows), bf16(3 * values_count, 2 * planes * rows)),
        [
            field_scratch, pltpu.VMEM((4 * MZ, NZ), jnp.bfloat16), *halves_scratch,
            pltpu.SemaphoreType.DMA((PIECES,)), pltpu.SemaphoreType.DMA((3,)),
        ],
        grid_field, table, far=(0, 1), limit=LARGE,
    )
    received, (wide, wide_back) = to_owner(
        kept, sent, (widen(local_weight), widen(local_weight.T))
    )

    def mix(*refs):
        mix_kernel(kyn, *refs)

    values, coef = call(
        mix, (given, coefs),
        [pltpu.VMEM((2, channels, modes), jnp.float32)] * 2 + [turn_scratch, pltpu.SemaphoreType.DMA],
        received, spectral_weight, plane_ahead, plane_back, out_specs=(VMEM, HBM),
    )
    def local_ahead(moved):
        _, late = lax.optimization_barrier((moved, wide))
        return call(local_kernel, f32(*grid_field.shape), [], grid_field, late)

    mine, other, local = from_owner(values, local_ahead)
    upstream, kept, sent = call(
        middle_kernel, (bf16(*grid_field.shape), sums, sums),
        halves_scratch,
        mine, other, local, row_back,
        jnp.asarray(depth_synthesis(pencils, True)), jnp.asarray(depth_analysis(pencils, True)), row_ahead,
    )
    received, local = to_owner(
        kept, sent, call(local_kernel, f32(*grid_field.shape), [], upstream, wide_back)
    )

    def unmix(*refs):
        unmix_kernel(kyn, *refs)

    values, back = call(
        unmix, (given, coefs), [turn_scratch],
        received, spectral_weight, plane_ahead, plane_back,
    )

    def outer(moved):
        _, late = lax.optimization_barrier((moved, back))
        return call(
            outer_kernel, f32(2, channels, channels, modes),
            [
                pltpu.VMEM((2, channels, channels, modes), jnp.float32),
                pltpu.SemaphoreType.DMA((2 * OUTER,)),
            ],
            coef, late, out_specs=HBM,
        )

    mine, other, grad_weight = from_owner(values, outer)
    grad_field = call(
        final_kernel, bf16(*grid_field.shape),
        [field_scratch, pltpu.SemaphoreType.DMA((OUTER,))],
        mine, other, local, row_back, jnp.asarray(depth_synthesis(pencils, False)),
        out_specs=HBM,
    )
    return grad_field, grad_weight


def solution(mesh):
    return jax.shard_map(
        on_device,
        mesh=mesh,
        in_specs=(P(None, "slab", "yz", None), P(None, None, None, ("slab", "yz")), P()),
        out_specs=(P(None, "slab", "yz", None), P(None, None, None, ("slab", "yz"))),
        check_vma=False,
    )
```

time: 66.6 us -> 63.5 us (0.953)
  Pallas kernels: 16.4 us -> 14.1 us
  local copies, waits for them, and re-layouts: 1.81 us -> 0.06 us
  waiting for transfers between devices: 0.01 us -> 1.22 us
    pallas_call x8, Pallas kernels: 16.4 us -> 14.1 us  [call(): pl.pallas_call(kernel, out_shape=outs, in_specs=[HBM if i in far else VME...]
    squeeze x1 -> x0, local copies, waits for them, and re-layouts: 0.91 us -> none  [on_device(): lax.dynamic_index_in_dim(jnp.asarray(row_synthesis(pencils, planes)), mem...]
    unnamed x26 -> x20, local copies, waits for them, and re-layouts: 0.91 us -> 0.06 us
    ppermute x2, waiting for transfers between devices: 0.01 us -> 0.81 us  [to_owner(): given = lax.ppermute(sent, 'yz', neighbours)]
  transfers between devices with their start and end apart: 4 -> 4, of which waited for: 0 -> 3; matrix products, arithmetic and copies ran while one was open for 3% -> 1% of each run, Pallas kernels for 6% -> 5%
where the time goes in v2:
time: 63.5 us; the launch traced here: 63.3 us
  blocking collectives  45.3 us (71%)
  Pallas kernels  14.1 us (22%)
  starting transfers between devices  1.23 us (2%)
  waiting for transfers between devices  1.22 us (2%)
  between operations  0.76 us (1%)
    all_to_all x2, blocking collectives, to_owner(): moved = lax.all_to_all(parts, ('slab', 'yz'), 0, 0, tiled=True)  25.2 us
    all_to_all x2, blocking collectives, from_owner(): moved = lax.all_to_all(values, ('slab', 'yz'), 0, 0, tiled=True)  20.1 us
    pallas_call x8, Pallas kernels, call(): pl.pallas_call(kernel, out_shape=outs, in_specs=[HBM if i in far else VME...  14.1 us
  transfers between devices with their start and end apart: 4, of which 3 were waited for; matrix products, arithmetic and copies ran while one was open for 1% of the time, Pallas kernels for 5%

profile of v2, /device:TPU:0, one launch (start us, length us, event | category | flops | bytes accessed | tf_op | source)
XLA Modules:
  0.0 63.3 jit_solution(7002054123872352466)
XLA Ops:
  0.6 0.0 copy-start
  0.6 0.0 copy-start.9
  0.7 0.0 copy-start.8
  0.7 0.0 copy-start.6
  0.7 0.0 copy-start.7
  0.7 0.0 copy-start.5
  0.7 3.0 %shard_map.122 = (f32[8,4,8,128]{3,2,1,0:T(8,128)S(1)}, f32[8,4,8,128]{3,2,1,0:T(8,128)S(1)}, bf16[128,256]{1,0:T(8,128)(2,1)S(1)}, bf16[192,256]{1,0:T(8,128)(2,1)S(1)}) custom-call(bf16[32,2,64,256]{3,2,1,0:T(8,128)(2,1)} %grid_ref.1, bf16[4,448,256]{2,1,0:T(8,128)(2,1)} %constant.16.clone.table_hbm), custom_call_target="tpu_custom_call" | custom-call | flops 1073741824 | bytes 4194304 | tf_op jit(solution)/shard_map/pallas_call | solution.py:411
  3.7 0.5 collective-permute-start
  4.3 0.0 copy-done.8
  4.3 0.3 fusion.1.wide_ref
  4.6 0.3 fusion.wide_ref
  4.9 0.4 collective-permute-done
  5.3 15.2 %all_to_all.20 = f32[32,8,128]{2,1,0:T(8,128)S(1)} all-to-all(f32[32,8,128]{2,1,0:T(8,128)S(1)} %bitcast.22), channel_id=1, replica_groups=mesh['slab'=8,'yz'=4] {'slab','yz'}, dimensions={0} | all-to-all | bytes 262144 | tf_op jit(solution)/shard_map/all_to_all | solution.py:464
  20.5 0.0 copy-done.7
  20.5 0.0 copy-start.1
  20.5 1.3 %shard_map.123 = (f32[8,4,8,128]{3,2,1,0:T(8,128)S(1)}, f32[2,32,256]{2,1,0:T(8,128)S(1)}) custom-call(f32[8,4,8,128]{3,2,1,0:T(8,128)S(1)} %bitcast.20, bf16[2,32,32,256]{3,2,1,0:T(8,128)(2,1)S(1)} %copy-done.5, bf16[192,128]{1,0:T(8,128)(2,1)S(1)} %copy-done.6, bf16[2,64,128]{2,1,0:T(8,128)(2,1)S(1)} %copy-done.7), custom_call_target="tpu_custom_call" | custom-call | flops 1073741824 | bytes 4194304 | tf_op jit(solution)/shard_map/pallas_call | solution.py:411
  21.9 10.0 %all_to_all.21 = f32[32,8,128]{2,1,0:T(8,128)S(1)} all-to-all(f32[32,8,128]{2,1,0:T(8,128)S(1)} %bitcast.21), channel_id=1, replica_groups=mesh['slab'=8,'yz'=4] {'slab','yz'}, dimensions={0} | all-to-all | bytes 262144 | tf_op jit(solution)/shard_map/all_to_all | solution.py:469
  31.9 0.2 collective-permute-start.1
  32.1 0.0 copy-done.1
  32.1 0.7 %shard_map.124.local_ref = f32[32,2,64,256]{3,2,1,0:T(8,128)S(1)} custom-call(bf16[32,2,64,256]{3,2,1,0:T(8,128)(2,1)S(1)} %copy-done.1, bf16[256,256]{1,0:T(8,128)(2,1)S(1)} %fusion.wide_ref), custom_call_target="tpu_custom_call" | custom-call | flops 1073741824 | bytes 4194304 | tf_op jit(solution)/shard_map/pallas_call | solution.py:411
  32.8 0.4 collective-permute-done.1.other_ref
  33.2 3.7 %shard_map.125 = (bf16[32,2,64,256]{3,2,1,0:T(8,128)(2,1)S(1)}, f32[8,4,8,128]{3,2,1,0:T(8,128)S(1)}, f32[8,4,8,128]{3,2,1,0:T(8,128)S(1)}) custom-call(f32[8,4,8,128]{3,2,1,0:T(8,128)S(1)} %bitcast.15, f32[8,4,8,128]{3,2,1,0:T(8,128)S(1)} %collective-permute-done.1.other_ref, f32[32,2,64,256]{3,2,1,0:T(8,128)S(1)} %shard_map.124.local_ref, ...), custom_call_target="tpu_custom_call" | custom-call | flops 1073741824 | bytes 4194304 | tf_op jit(solution)/shard_map/pallas_call | solution.py:411
  37.0 0.3 collective-permute-start.2
  37.2 0.7 %shard_map.126.local_ref = f32[32,2,64,256]{3,2,1,0:T(8,128)S(1)} custom-call(bf16[32,2,64,256]{3,2,1,0:T(8,128)(2,1)S(1)} %get-tuple-element.39.grid_ref, bf16[256,256]{1,0:T(8,128)(2,1)S(1)} %fusion.1.wide_ref), custom_call_target="tpu_custom_call" | custom-call | flops 1073741824 | bytes 4194304 | tf_op jit(solution)/shard_map/pallas_call | solution.py:411
  38.0 0.4 collective-permute-done.2
  38.4 10.0 %all_to_all.22 = f32[32,8,128]{2,1,0:T(8,128)S(1)} all-to-all(f32[32,8,128]{2,1,0:T(8,128)S(1)} %bitcast.23), channel_id=1, replica_groups=mesh['slab'=8,'yz'=4] {'slab','yz'}, dimensions={0} | all-to-all | bytes 262144 | tf_op jit(solution)/shard_map/all_to_all | solution.py:464
  48.4 1.1 %shard_map.127 = (f32[8,4,8,128]{3,2,1,0:T(8,128)S(1)}, f32[2,32,256]{2,1,0:T(8,128)S(1)}) custom-call(f32[8,4,8,128]{3,2,1,0:T(8,128)S(1)} %bitcast.18, bf16[2,32,32,256]{3,2,1,0:T(8,128)(2,1)S(1)} %copy-done.5, bf16[192,128]{1,0:T(8,128)(2,1)S(1)} %copy-done.6, bf16[2,64,128]{2,1,0:T(8,128)(2,1)S(1)} %copy-done.7), custom_call_target="tpu_custom_call" | custom-call | flops 1073741824 | bytes 4194304 | tf_op jit(solution)/shard_map/pallas_call | solution.py:411
  49.5 10.1 %all_to_all.23 = f32[32,8,128]{2,1,0:T(8,128)S(1)} all-to-all(f32[32,8,128]{2,1,0:T(8,128)S(1)} %bitcast.19), channel_id=1, replica_groups=mesh['slab'=8,'yz'=4] {'slab','yz'}, dimensions={0} | all-to-all | bytes 262144 | tf_op jit(solution)/shard_map/all_to_all | solution.py:469
  59.6 0.2 collective-permute-start.3
  59.8 1.4 %shard_map.128 = f32[2,32,32,256]{3,2,1,0:T(8,128)} custom-call(f32[2,32,256]{2,1,0:T(8,128)S(1)} %get-tuple-element.43.coef_ref, f32[2,32,256]{2,1,0:T(8,128)S(1)} %get-tuple-element.45.back_ref), custom_call_target="tpu_custom_call" | custom-call | flops 1073741824 | bytes 4194304 | tf_op jit(solution)/shard_map/pallas_call | solution.py:411
  61.2 0.0 collective-permute-done.3.other_ref
  61.3 2.0 %shard_map.129 = bf16[32,2,64,256]{3,2,1,0:T(8,128)(2,1)} custom-call(f32[8,4,8,128]{3,2,1,0:T(8,128)S(1)} %bitcast.17, f32[8,4,8,128]{3,2,1,0:T(8,128)S(1)} %collective-permute-done.3.other_ref, f32[32,2,64,256]{3,2,1,0:T(8,128)S(1)} %shard_map.126.local_ref, bf16[192,256]{1,0:T(8,128)(2,1)S(1)} %get-tuple-element.35.lift_ref, bf16[128,256]{1,0:T(8,128)(2,1)S(1)} %copy-done.2), custom_call_target="tpu_custom_call" | custom-call | flops 1073741824 | bytes 4194304 | tf_op jit(solution)/shard_map/pallas_call | solution.py:411
  (12 shorter events, 0.1 us)
Async XLA Ops:
  0.6 3.6 %copy-start = (bf16[32,32]{1,0:T(8,128)(2,1)S(1)}, bf16[32,32]{1,0:T(8,128)(2,1)}, u32[]{:S(2)}) copy-start(bf16[32,32]{1,0:T(8,128)(2,1)} %param.13) | copy-start | bytes 6148
  0.6 3.6 %copy-start.9 = (bf16[256,256]{1,0:T(8,128)(2,1)S(1)}, bf16[256,256]{1,0:T(8,128)(2,1)}, u32[]{:S(2)}) copy-start(bf16[256,256]{1,0:T(8,128)(2,1)} %constant.20.clone) | copy-start | bytes 393220
  0.7 3.6 %copy-start.8 = (bf16[256,32]{1,0:T(8,128)(2,1)S(1)}, bf16[256,32]{1,0:T(8,128)(2,1)}, u32[]{:S(2)}) copy-start(bf16[256,32]{1,0:T(8,128)(2,1)} %constant.19.clone) | copy-start | bytes 49156
  0.7 19.8 %copy-start.6 = (bf16[192,128]{1,0:T(8,128)(2,1)S(1)}, bf16[192,128]{1,0:T(8,128)(2,1)}, u32[]{:S(2)}) copy-start(bf16[192,128]{1,0:T(8,128)(2,1)} %constant.17.clone.refs_2_) | copy-start | bytes 147460
  0.7 19.8 %copy-start.7 = (bf16[2,64,128]{2,1,0:T(8,128)(2,1)S(1)}, bf16[2,64,128]{2,1,0:T(8,128)(2,1)}, u32[]{:S(2)}) copy-start(bf16[2,64,128]{2,1,0:T(8,128)(2,1)} %constant.18.clone.refs_3_) | copy-start | bytes 98308
  0.7 19.8 %copy-start.5 = (bf16[2,32,32,256]{3,2,1,0:T(8,128)(2,1)S(1)}, bf16[2,32,32,256]{3,2,1,0:T(8,128)(2,1)}, u32[]{:S(2)}) copy-start(bf16[2,32,32,256]{3,2,1,0:T(8,128)(2,1)} %refs_1_.3) | copy-start | bytes 3145732
  3.7 1.5 %collective-permute-start = (f32[8,4,8,128]{3,2,1,0:T(8,128)S(1)}, f32[8,4,8,128]{3,2,1,0:T(8,128)S(1)}, u32[]{:S(2)}, u32[]{:S(2)}) collective-permute-start(f32[8,4,8,128]{3,2,1,0:T(8,128)S(1)} %get-tuple-element.27), channel_id=1, source_target_pairs={{0,1},{1,0},{2,3},{3,2},{4,5},{5,4},{6,7},{7,6},{8,9},{9,8},{10,11... | collective-permute-start | bytes 393224 | tf_op jit(solution)/shard_map/ppermute | solution.py:457
  20.5 11.6 %copy-start.1 = (bf16[32,2,64,256]{3,2,1,0:T(8,128)(2,1)S(1)}, bf16[32,2,64,256]{3,2,1,0:T(8,128)(2,1)}, u32[]{:S(2)}) copy-start(bf16[32,2,64,256]{3,2,1,0:T(8,128)(2,1)} %grid_ref.1) | copy-start | bytes 6291460
  31.9 1.4 %copy-start.3 = (bf16[128,256]{1,0:T(8,128)(2,1)S(1)}, bf16[128,256]{1,0:T(8,128)(2,1)}, u32[]{:S(2)}) copy-start(bf16[128,256]{1,0:T(8,128)(2,1)} %constant.22.clone.depth_ref) | copy-start | bytes 196612
  31.9 1.4 %copy-start.4 = (bf16[128,256]{1,0:T(8,128)(2,1)S(1)}, bf16[128,256]{1,0:T(8,128)(2,1)}, u32[]{:S(2)}) copy-start(bf16[128,256]{1,0:T(8,128)(2,1)} %constant.21.clone.synth_ref) | copy-start | bytes 196612
  31.9 1.3 %collective-permute-start.1 = (f32[8,4,8,128]{3,2,1,0:T(8,128)S(1)}, f32[8,4,8,128]{3,2,1,0:T(8,128)S(1)}, u32[]{:S(2)}, u32[]{:S(2)}) collective-permute-start(f32[8,4,8,128]{3,2,1,0:T(8,128)S(1)} %bitcast.14), channel_id=1, source_target_pairs={{0,1},{1,0},{2,3},{3,2},{4,5},{5,4},{6,7},{7,6},{8,9},{9,8},{10,11... | collective-permute-start | bytes 393224 | tf_op jit(solution)/shard_map/ppermute | solution.py:474
  37.0 1.4 %collective-permute-start.2 = (f32[8,4,8,128]{3,2,1,0:T(8,128)S(1)}, f32[8,4,8,128]{3,2,1,0:T(8,128)S(1)}, u32[]{:S(2)}, u32[]{:S(2)}) collective-permute-start(f32[8,4,8,128]{3,2,1,0:T(8,128)S(1)} %get-tuple-element.38), channel_id=1, source_target_pairs={{0,1},{1,0},{2,3},{3,2},{4,5},{5,4},{6,7},{7,6},{8,9},{9,8},{10,11... | collective-permute-start | bytes 393224 | tf_op jit(solution)/shard_map/ppermute | solution.py:457
  49.5 11.7 %copy-start.2 = (bf16[128,256]{1,0:T(8,128)(2,1)S(1)}, bf16[128,256]{1,0:T(8,128)(2,1)}, u32[]{:S(2)}) copy-start(bf16[128,256]{1,0:T(8,128)(2,1)} %constant.23.clone.synth_ref) | copy-start | bytes 196612
  59.6 1.7 %collective-permute-start.3 = (f32[8,4,8,128]{3,2,1,0:T(8,128)S(1)}, f32[8,4,8,128]{3,2,1,0:T(8,128)S(1)}, u32[]{:S(2)}, u32[]{:S(2)}) collective-permute-start(f32[8,4,8,128]{3,2,1,0:T(8,128)S(1)} %bitcast.16), channel_id=1, source_target_pairs={{0,1},{1,0},{2,3},{3,2},{4,5},{5,4},{6,7},{7,6},{8,9},{9,8},{10,11... | collective-permute-start | bytes 393224 | tf_op jit(solution)/shard_map/ppermute | solution.py:474

commit v3 on v2

--- a/solution.py
+++ b/solution.py
@@ -180,9 +180,9 @@
         sent_ref[:, q] = jnp.where(first, high, low)
 
 
-def fetch(hbm, ref, sem):
+def fetch(hbm, ref, sem, lane=0):
     copy = pltpu.make_async_copy(hbm, ref, sem)
-    copy.start()
+    copy.start(priority=lane)
     return copy
 
 
@@ -197,7 +197,7 @@
     second = first + row_ref.shape[0]
     depth_copy = fetch(table.at[pl.ds(0, first)], depth_ref, table_sem.at[0])
     pieces = [
-        fetch(grid_hbm.at[pl.ds(i * step, step)], grid_ref.at[pl.ds(i * step, step)], piece_sem.at[i])
+        fetch(grid_hbm.at[pl.ds(i * step, step)], grid_ref.at[pl.ds(i * step, step)], piece_sem.at[i], i % 2)
         for i in range(PIECES)
     ]
     row_copy = fetch(table.at[pl.ds(first, row_ref.shape[0])], row_ref, table_sem.at[1])
@@ -296,28 +296,13 @@
     distribute(modes_real, modes_imag, back_ref, turn_ref, kyn, out_ref)
 
 
-def outer_kernel(coef_ref, back_ref, out_hbm, out_ref, sems):
+def outer_kernel(coef_ref, back_ref, out_ref):
     real, imag = coef_ref[0], coef_ref[1]
-    channels = back_ref.shape[1]
-    step = channels // OUTER
-    copies = []
-    for o in range(channels):
+    for o in range(back_ref.shape[1]):
         back_real = back_ref[0, o : o + 1]
         back_imag = back_ref[1, o : o + 1]
         out_ref[0, o] = back_real * real + back_imag * imag
         out_ref[1, o] = back_imag * real - back_real * imag
-        if (o + 1) % step == 0:
-            start = o + 1 - step
-            for part in range(2):
-                copies.append(
-                    fetch(
-                        out_ref.at[part, pl.ds(start, step)],
-                        out_hbm.at[part, pl.ds(start, step)],
-                        sems.at[len(copies)],
-                    )
-                )
-    for copy in copies:
-        copy.wait()
 
 
 def lift(mine_ref, other_ref, row_ref):
@@ -386,9 +371,11 @@
 
 
 def final_kernel(
-    mine_ref, other_ref, local_ref, lift_ref, synth_ref, out_hbm, result_ref, out_sems
+    mine_ref, other_ref, local_ref, lift_ref, synth_ref, product_ref, out_hbm, weight_hbm,
+    result_ref, out_sems, weight_sem,
 ):
     channels, planes, rows, cells = local_ref.shape
+    weight_copy = fetch(product_ref, weight_hbm, weight_sem, 1)
     lines = lift(mine_ref, other_ref, lift_ref)
     step = channels // OUTER
     copies = []
@@ -399,7 +386,7 @@
         if (o + 1) % step == 0:
             part = pl.ds(o + 1 - step, step)
             copies.append(fetch(result_ref.at[part], out_hbm.at[part], out_sems.at[len(copies)]))
-    for copy in copies:
+    for copy in [weight_copy] + copies:
         copy.wait()
 
 
@@ -529,23 +516,15 @@
 
     def outer(moved):
         _, late = lax.optimization_barrier((moved, back))
-        return call(
-            outer_kernel, f32(2, channels, channels, modes),
-            [
-                pltpu.VMEM((2, channels, channels, modes), jnp.float32),
-                pltpu.SemaphoreType.DMA((2 * OUTER,)),
-            ],
-            coef, late, out_specs=HBM,
-        )
-
-    mine, other, grad_weight = from_owner(values, outer)
-    grad_field = call(
-        final_kernel, bf16(*grid_field.shape),
-        [field_scratch, pltpu.SemaphoreType.DMA((OUTER,))],
-        mine, other, local, row_back, jnp.asarray(depth_synthesis(pencils, False)),
-        out_specs=HBM,
-    )
-    return grad_field, grad_weight
+        return call(outer_kernel, f32(2, channels, channels, modes), [], coef, late)
+
+    mine, other, products = from_owner(values, outer)
+    return call(
+        final_kernel, (bf16(*grid_field.shape), f32(2, channels, channels, modes)),
+        [field_scratch, pltpu.SemaphoreType.DMA((OUTER,)), pltpu.SemaphoreType.DMA],
+        mine, other, local, row_back, jnp.asarray(depth_synthesis(pencils, False)), products,
+        out_specs=(HBM, HBM),
+    )
 
 
 def solution(mesh):

time: 63.5 us -> 63 us (level)
  Pallas kernels: 14.1 us -> 12.7 us
  waiting for transfers between devices: 1.22 us -> 2.13 us
    pallas_call x8, Pallas kernels: 14.1 us -> 12.7 us  [call(): pl.pallas_call(kernel, out_shape=outs, in_specs=[HBM if i in far else VME...]
    ppermute x2, waiting for transfers between devices: 0.42 us -> 1.32 us  [from_owner(): other = lax.ppermute(moved, 'yz', neighbours)]
  transfers between devices with their start and end apart: 4 -> 4, of which waited for: 3 -> 4; matrix products, arithmetic and copies ran while one was open for 1% -> 1% of each run, Pallas kernels for 5% -> 3%
where the time goes in v3:
time: 63 us; the launch traced here: 62.7 us
  blocking collectives  45.3 us (72%)
  Pallas kernels  12.7 us (20%)
  waiting for transfers between devices  2.13 us (3%)
  starting transfers between devices  1.24 us (2%)
  between operations  0.74 us (1%)
    all_to_all x2, blocking collectives, to_owner(): moved = lax.all_to_all(parts, ('slab', 'yz'), 0, 0, tiled=True)  25.2 us
    all_to_all x2, blocking collectives, from_owner(): moved = lax.all_to_all(values, ('slab', 'yz'), 0, 0, tiled=True)  20.1 us
    pallas_call x8, Pallas kernels, call(): pl.pallas_call(kernel, out_shape=outs, in_specs=[HBM if i in far else VME...  12.7 us
    ppermute x2, waiting for transfers between devices, from_owner(): other = lax.ppermute(moved, 'yz', neighbours)  1.32 us
  transfers between devices with their start and end apart: 4, of which 4 were waited for; matrix products, arithmetic and copies ran while one was open for 1% of the time, Pallas kernels for 3%

profile of v3, /device:TPU:0, one launch (start us, length us, event | category | flops | bytes accessed | tf_op | source)
XLA Modules:
  0.0 62.7 jit_solution(4756655613927434417)
XLA Ops:
  0.6 0.0 copy-start
  0.6 0.0 copy-start.9
  0.7 0.0 copy-start.8
  0.7 0.0 copy-start.6
  0.7 0.0 copy-start.7
  0.7 2.8 %shard_map.122 = (f32[8,4,8,128]{3,2,1,0:T(8,128)S(1)}, f32[8,4,8,128]{3,2,1,0:T(8,128)S(1)}, bf16[128,256]{1,0:T(8,128)(2,1)S(1)}, bf16[192,256]{1,0:T(8,128)(2,1)S(1)}) custom-call(bf16[32,2,64,256]{3,2,1,0:T(8,128)(2,1)} %grid_ref.1, bf16[4,448,256]{2,1,0:T(8,128)(2,1)} %constant.16.clone.table_hbm), custom_call_target="tpu_custom_call" | custom-call | flops 1073741824 | bytes 4194304 | tf_op jit(solution)/shard_map/pallas_call | solution.py:398
  3.5 0.5 collective-permute-start
  4.0 0.0 copy-done
  4.0 0.0 copy-done.8
  4.0 0.3 fusion.1.wide_ref
  4.3 0.3 fusion.wide_ref
  4.6 0.4 collective-permute-done
  5.0 15.2 %all_to_all.20 = f32[32,8,128]{2,1,0:T(8,128)S(1)} all-to-all(f32[32,8,128]{2,1,0:T(8,128)S(1)} %bitcast.22), channel_id=1, replica_groups=mesh['slab'=8,'yz'=4] {'slab','yz'}, dimensions={0} | all-to-all | bytes 262144 | tf_op jit(solution)/shard_map/all_to_all | solution.py:451
  20.3 0.0 copy-done.7
  20.3 0.0 copy-start.1
  20.3 1.3 %shard_map.123 = (f32[8,4,8,128]{3,2,1,0:T(8,128)S(1)}, f32[2,32,256]{2,1,0:T(8,128)S(1)}) custom-call(f32[8,4,8,128]{3,2,1,0:T(8,128)S(1)} %bitcast.20, bf16[2,32,32,256]{3,2,1,0:T(8,128)(2,1)S(1)} %copy-done.5, bf16[192,128]{1,0:T(8,128)(2,1)S(1)} %copy-done.6, bf16[2,64,128]{2,1,0:T(8,128)(2,1)S(1)} %copy-done.7), custom_call_target="tpu_custom_call" | custom-call | flops 1073741824 | bytes 4194304 | tf_op jit(solution)/shard_map/pallas_call | solution.py:398
  21.6 10.0 %all_to_all.21 = f32[32,8,128]{2,1,0:T(8,128)S(1)} all-to-all(f32[32,8,128]{2,1,0:T(8,128)S(1)} %bitcast.21), channel_id=1, replica_groups=mesh['slab'=8,'yz'=4] {'slab','yz'}, dimensions={0} | all-to-all | bytes 262144 | tf_op jit(solution)/shard_map/all_to_all | solution.py:456
  31.6 0.2 collective-permute-start.1
  31.8 0.0 copy-done.1
  31.8 0.7 %shard_map.124.local_ref = f32[32,2,64,256]{3,2,1,0:T(8,128)S(1)} custom-call(bf16[32,2,64,256]{3,2,1,0:T(8,128)(2,1)S(1)} %copy-done.1, bf16[256,256]{1,0:T(8,128)(2,1)S(1)} %fusion.wide_ref), custom_call_target="tpu_custom_call" | custom-call | flops 1073741824 | bytes 4194304 | tf_op jit(solution)/shard_map/pallas_call | solution.py:398
  32.6 0.4 collective-permute-done.1.other_ref
  33.0 3.7 %shard_map.125 = (bf16[32,2,64,256]{3,2,1,0:T(8,128)(2,1)S(1)}, f32[8,4,8,128]{3,2,1,0:T(8,128)S(1)}, f32[8,4,8,128]{3,2,1,0:T(8,128)S(1)}) custom-call(f32[8,4,8,128]{3,2,1,0:T(8,128)S(1)} %bitcast.17, f32[8,4,8,128]{3,2,1,0:T(8,128)S(1)} %collective-permute-done.1.other_ref, f32[32,2,64,256]{3,2,1,0:T(8,128)S(1)} %shard_map.124.local_ref, ...), custom_call_target="tpu_custom_call" | custom-call | flops 1073741824 | bytes 4194304 | tf_op jit(solution)/shard_map/pallas_call | solution.py:398
  36.7 0.3 collective-permute-start.2
  37.0 0.7 %shard_map.126.local_ref = f32[32,2,64,256]{3,2,1,0:T(8,128)S(1)} custom-call(bf16[32,2,64,256]{3,2,1,0:T(8,128)(2,1)S(1)} %get-tuple-element.39.grid_ref, bf16[256,256]{1,0:T(8,128)(2,1)S(1)} %fusion.1.wide_ref), custom_call_target="tpu_custom_call" | custom-call | flops 1073741824 | bytes 4194304 | tf_op jit(solution)/shard_map/pallas_call | solution.py:398
  37.7 0.4 collective-permute-done.2
  38.2 10.0 %all_to_all.22 = f32[32,8,128]{2,1,0:T(8,128)S(1)} all-to-all(f32[32,8,128]{2,1,0:T(8,128)S(1)} %bitcast.23), channel_id=1, replica_groups=mesh['slab'=8,'yz'=4] {'slab','yz'}, dimensions={0} | all-to-all | bytes 262144 | tf_op jit(solution)/shard_map/all_to_all | solution.py:451
  48.2 1.1 %shard_map.127 = (f32[8,4,8,128]{3,2,1,0:T(8,128)S(1)}, f32[2,32,256]{2,1,0:T(8,128)S(1)}) custom-call(f32[8,4,8,128]{3,2,1,0:T(8,128)S(1)} %bitcast.18, bf16[2,32,32,256]{3,2,1,0:T(8,128)(2,1)S(1)} %copy-done.5, bf16[192,128]{1,0:T(8,128)(2,1)S(1)} %copy-done.6, bf16[2,64,128]{2,1,0:T(8,128)(2,1)S(1)} %copy-done.7), custom_call_target="tpu_custom_call" | custom-call | flops 1073741824 | bytes 4194304 | tf_op jit(solution)/shard_map/pallas_call | solution.py:398
  49.3 10.1 %all_to_all.23 = f32[32,8,128]{2,1,0:T(8,128)S(1)} all-to-all(f32[32,8,128]{2,1,0:T(8,128)S(1)} %bitcast.19), channel_id=1, replica_groups=mesh['slab'=8,'yz'=4] {'slab','yz'}, dimensions={0} | all-to-all | bytes 262144 | tf_op jit(solution)/shard_map/all_to_all | solution.py:456
  59.3 0.2 collective-permute-start.3
  59.5 0.2 shard_map.128.product_ref
  59.8 0.9 %collective-permute-done.3.other_ref = f32[8,4,8,128]{3,2,1,0:T(8,128)S(1)} collective-permute-done((f32[8,4,8,128]{3,2,1,0:T(8,128)S(1)}, f32[8,4,8,128]{3,2,1,0:T(8,128)S(1)}, u32[]{:S(2)}, u32[]{:S(2)}) %collective-permute-start.3) | collective-permute-done | bytes 131104 | tf_op jit(solution)/shard_map/ppermute | solution.py:461
  60.7 2.1 %shard_map.129 = (bf16[32,2,64,256]{3,2,1,0:T(8,128)(2,1)}, f32[2,32,32,256]{3,2,1,0:T(8,128)}) custom-call(f32[8,4,8,128]{3,2,1,0:T(8,128)S(1)} %bitcast.15, f32[8,4,8,128]{3,2,1,0:T(8,128)S(1)} %collective-permute-done.3.other_ref, f32[32,2,64,256]{3,2,1,0:T(8,128)S(1)} %shard_map.126.local_ref, bf16[192,256]{1,0:T(8,128)(2,1)S(1)} %get-tuple-element.35.lift_ref, ...), custom_call_target="tpu_custom_call" | custom-call | flops 1073741824 | bytes 4194304 | tf_op jit(solution)/shard_map/pallas_call | solution.py:398
  (12 shorter events, 0.1 us)
Async XLA Ops:
  0.6 3.4 %copy-start = (bf16[32,32]{1,0:T(8,128)(2,1)S(1)}, bf16[32,32]{1,0:T(8,128)(2,1)}, u32[]{:S(2)}) copy-start(bf16[32,32]{1,0:T(8,128)(2,1)} %param.13) | copy-start | bytes 6148
  0.6 3.4 %copy-start.9 = (bf16[256,256]{1,0:T(8,128)(2,1)S(1)}, bf16[256,256]{1,0:T(8,128)(2,1)}, u32[]{:S(2)}) copy-start(bf16[256,256]{1,0:T(8,128)(2,1)} %constant.20.clone) | copy-start | bytes 393220
  0.7 3.4 %copy-start.8 = (bf16[256,32]{1,0:T(8,128)(2,1)S(1)}, bf16[256,32]{1,0:T(8,128)(2,1)}, u32[]{:S(2)}) copy-start(bf16[256,32]{1,0:T(8,128)(2,1)} %constant.19.clone) | copy-start | bytes 49156
  0.7 19.6 %copy-start.6 = (bf16[192,128]{1,0:T(8,128)(2,1)S(1)}, bf16[192,128]{1,0:T(8,128)(2,1)}, u32[]{:S(2)}) copy-start(bf16[192,128]{1,0:T(8,128)(2,1)} %constant.17.clone.refs_2_) | copy-start | bytes 147460
  0.7 19.6 %copy-start.7 = (bf16[2,64,128]{2,1,0:T(8,128)(2,1)S(1)}, bf16[2,64,128]{2,1,0:T(8,128)(2,1)}, u32[]{:S(2)}) copy-start(bf16[2,64,128]{2,1,0:T(8,128)(2,1)} %constant.18.clone.refs_3_) | copy-start | bytes 98308
  0.7 19.6 %copy-start.5 = (bf16[2,32,32,256]{3,2,1,0:T(8,128)(2,1)S(1)}, bf16[2,32,32,256]{3,2,1,0:T(8,128)(2,1)}, u32[]{:S(2)}) copy-start(bf16[2,32,32,256]{3,2,1,0:T(8,128)(2,1)} %refs_1_.3) | copy-start | bytes 3145732
  3.5 1.5 %collective-permute-start = (f32[8,4,8,128]{3,2,1,0:T(8,128)S(1)}, f32[8,4,8,128]{3,2,1,0:T(8,128)S(1)}, u32[]{:S(2)}, u32[]{:S(2)}) collective-permute-start(f32[8,4,8,128]{3,2,1,0:T(8,128)S(1)} %get-tuple-element.27), channel_id=1, source_target_pairs={{0,1},{1,0},{2,3},{3,2},{4,5},{5,4},{6,7},{7,6},{8,9},{9,8},{10,11... | collective-permute-start | bytes 393224 | tf_op jit(solution)/shard_map/ppermute | solution.py:444
  20.3 11.6 %copy-start.1 = (bf16[32,2,64,256]{3,2,1,0:T(8,128)(2,1)S(1)}, bf16[32,2,64,256]{3,2,1,0:T(8,128)(2,1)}, u32[]{:S(2)}) copy-start(bf16[32,2,64,256]{3,2,1,0:T(8,128)(2,1)} %grid_ref.1) | copy-start | bytes 6291460
  31.6 1.4 %copy-start.3 = (bf16[128,256]{1,0:T(8,128)(2,1)S(1)}, bf16[128,256]{1,0:T(8,128)(2,1)}, u32[]{:S(2)}) copy-start(bf16[128,256]{1,0:T(8,128)(2,1)} %constant.22.clone.depth_ref) | copy-start | bytes 196612
  31.6 1.4 %copy-start.4 = (bf16[128,256]{1,0:T(8,128)(2,1)S(1)}, bf16[128,256]{1,0:T(8,128)(2,1)}, u32[]{:S(2)}) copy-start(bf16[128,256]{1,0:T(8,128)(2,1)} %constant.21.clone.synth_ref) | copy-start | bytes 196612
  31.6 1.3 %collective-permute-start.1 = (f32[8,4,8,128]{3,2,1,0:T(8,128)S(1)}, f32[8,4,8,128]{3,2,1,0:T(8,128)S(1)}, u32[]{:S(2)}, u32[]{:S(2)}) collective-permute-start(f32[8,4,8,128]{3,2,1,0:T(8,128)S(1)} %bitcast.16), channel_id=1, source_target_pairs={{0,1},{1,0},{2,3},{3,2},{4,5},{5,4},{6,7},{7,6},{8,9},{9,8},{10,11... | collective-permute-start | bytes 393224 | tf_op jit(solution)/shard_map/ppermute | solution.py:461
  36.7 1.4 %collective-permute-start.2 = (f32[8,4,8,128]{3,2,1,0:T(8,128)S(1)}, f32[8,4,8,128]{3,2,1,0:T(8,128)S(1)}, u32[]{:S(2)}, u32[]{:S(2)}) collective-permute-start(f32[8,4,8,128]{3,2,1,0:T(8,128)S(1)} %get-tuple-element.38), channel_id=1, source_target_pairs={{0,1},{1,0},{2,3},{3,2},{4,5},{5,4},{6,7},{7,6},{8,9},{9,8},{10,11... | collective-permute-start | bytes 393224 | tf_op jit(solution)/shard_map/ppermute | solution.py:444
  49.3 11.4 %copy-start.2 = (bf16[128,256]{1,0:T(8,128)(2,1)S(1)}, bf16[128,256]{1,0:T(8,128)(2,1)}, u32[]{:S(2)}) copy-start(bf16[128,256]{1,0:T(8,128)(2,1)} %constant.23.clone.synth_ref) | copy-start | bytes 196612
  59.3 1.3 %collective-permute-start.3 = (f32[8,4,8,128]{3,2,1,0:T(8,128)S(1)}, f32[8,4,8,128]{3,2,1,0:T(8,128)S(1)}, u32[]{:S(2)}, u32[]{:S(2)}) collective-permute-start(f32[8,4,8,128]{3,2,1,0:T(8,128)S(1)} %bitcast.14), channel_id=1, source_target_pairs={{0,1},{1,0},{2,3},{3,2},{4,5},{5,4},{6,7},{7,6},{8,9},{9,8},{10,11... | collective-permute-start | bytes 393224 | tf_op jit(solution)/shard_map/ppermute | solution.py:461

commit v4 on v3

--- a/solution.py
+++ b/solution.py
@@ -332,8 +332,7 @@
         ],
         axis=0,
     )
-    upper = block.astype(jnp.bfloat16).astype(jnp.float32)
-    return jnp.concatenate([upper, block - upper], axis=0).T.astype(jnp.bfloat16)
+    return jnp.concatenate(split(block), axis=0).T
 
 
 def local_kernel(grid_ref, wide_ref, out_ref):

time: 63 us -> 62.8 us (level)
  no operation moved by 1% of the time
where the time goes in v4:
time: 62.8 us; the launch traced here: 62.6 us
  blocking collectives  45.3 us (72%)
  Pallas kernels  12.5 us (20%)
  waiting for transfers between devices  2.13 us (3%)
  starting transfers between devices  1.24 us (2%)
  between operations  0.75 us (1%)
    all_to_all x2, blocking collectives, to_owner(): moved = lax.all_to_all(parts, ('slab', 'yz'), 0, 0, tiled=True)  25.2 us
    all_to_all x2, blocking collectives, from_owner(): moved = lax.all_to_all(values, ('slab', 'yz'), 0, 0, tiled=True)  20.1 us
    pallas_call x8, Pallas kernels, call(): pl.pallas_call(kernel, out_shape=outs, in_specs=[HBM if i in far else VME...  12.5 us
    ppermute x2, waiting for transfers between devices, from_owner(): other = lax.ppermute(moved, 'yz', neighbours)  1.32 us
  transfers between devices with their start and end apart: 4, of which 4 were waited for; matrix products, arithmetic and copies ran while one was open for 1% of the time, Pallas kernels for 3%

profile of v4, /device:TPU:0, one launch (start us, length us, event | category | flops | bytes accessed | tf_op | source)
XLA Modules:
  0.0 62.6 jit_solution(14580588567353678997)
XLA Ops:
  0.6 0.0 copy-start
  0.6 0.0 copy-start.9
  0.7 0.0 copy-start.8
  0.7 0.0 copy-start.6
  0.7 0.0 copy-start.7
  0.7 2.8 %shard_map.122 = (f32[8,4,8,128]{3,2,1,0:T(8,128)S(1)}, f32[8,4,8,128]{3,2,1,0:T(8,128)S(1)}, bf16[128,256]{1,0:T(8,128)(2,1)S(1)}, bf16[192,256]{1,0:T(8,128)(2,1)S(1)}) custom-call(bf16[32,2,64,256]{3,2,1,0:T(8,128)(2,1)} %grid_ref.1, bf16[4,448,256]{2,1,0:T(8,128)(2,1)} %constant.16.clone.table_hbm), custom_call_target="tpu_custom_call" | custom-call | flops 1073741824 | bytes 4194304 | tf_op jit(solution)/shard_map/pallas_call | solution.py:397
  3.5 0.5 collective-permute-start
  4.0 0.0 copy-done
  4.0 0.0 copy-done.8
  4.0 0.3 fusion.1.wide_ref
  4.3 0.3 fusion.wide_ref
  4.6 0.4 collective-permute-done
  5.0 15.2 %all_to_all.20 = f32[32,8,128]{2,1,0:T(8,128)S(1)} all-to-all(f32[32,8,128]{2,1,0:T(8,128)S(1)} %bitcast.22), channel_id=1, replica_groups=mesh['slab'=8,'yz'=4] {'slab','yz'}, dimensions={0} | all-to-all | bytes 262144 | tf_op jit(solution)/shard_map/all_to_all | solution.py:450
  20.3 0.0 copy-done.7
  20.3 0.0 copy-start.1
  20.3 1.3 %shard_map.123 = (f32[8,4,8,128]{3,2,1,0:T(8,128)S(1)}, f32[2,32,256]{2,1,0:T(8,128)S(1)}) custom-call(f32[8,4,8,128]{3,2,1,0:T(8,128)S(1)} %bitcast.20, bf16[2,32,32,256]{3,2,1,0:T(8,128)(2,1)S(1)} %copy-done.5, bf16[192,128]{1,0:T(8,128)(2,1)S(1)} %copy-done.6, bf16[2,64,128]{2,1,0:T(8,128)(2,1)S(1)} %copy-done.7), custom_call_target="tpu_custom_call" | custom-call | flops 1073741824 | bytes 4194304 | tf_op jit(solution)/shard_map/pallas_call | solution.py:397
  21.6 10.0 %all_to_all.21 = f32[32,8,128]{2,1,0:T(8,128)S(1)} all-to-all(f32[32,8,128]{2,1,0:T(8,128)S(1)} %bitcast.21), channel_id=1, replica_groups=mesh['slab'=8,'yz'=4] {'slab','yz'}, dimensions={0} | all-to-all | bytes 262144 | tf_op jit(solution)/shard_map/all_to_all | solution.py:455
  31.6 0.2 collective-permute-start.1
  31.8 0.0 copy-done.1
  31.8 0.7 %shard_map.124.local_ref = f32[32,2,64,256]{3,2,1,0:T(8,128)S(1)} custom-call(bf16[32,2,64,256]{3,2,1,0:T(8,128)(2,1)S(1)} %copy-done.1, bf16[256,256]{1,0:T(8,128)(2,1)S(1)} %fusion.wide_ref), custom_call_target="tpu_custom_call" | custom-call | flops 1073741824 | bytes 4194304 | tf_op jit(solution)/shard_map/pallas_call | solution.py:397
  32.6 0.4 collective-permute-done.1.other_ref
  33.0 3.6 %shard_map.125 = (bf16[32,2,64,256]{3,2,1,0:T(8,128)(2,1)S(1)}, f32[8,4,8,128]{3,2,1,0:T(8,128)S(1)}, f32[8,4,8,128]{3,2,1,0:T(8,128)S(1)}) custom-call(f32[8,4,8,128]{3,2,1,0:T(8,128)S(1)} %bitcast.17, f32[8,4,8,128]{3,2,1,0:T(8,128)S(1)} %collective-permute-done.1.other_ref, f32[32,2,64,256]{3,2,1,0:T(8,128)S(1)} %shard_map.124.local_ref, ...), custom_call_target="tpu_custom_call" | custom-call | flops 1073741824 | bytes 4194304 | tf_op jit(solution)/shard_map/pallas_call | solution.py:397
  36.6 0.3 collective-permute-start.2
  36.9 0.7 %shard_map.126.local_ref = f32[32,2,64,256]{3,2,1,0:T(8,128)S(1)} custom-call(bf16[32,2,64,256]{3,2,1,0:T(8,128)(2,1)S(1)} %get-tuple-element.39.grid_ref, bf16[256,256]{1,0:T(8,128)(2,1)S(1)} %fusion.1.wide_ref), custom_call_target="tpu_custom_call" | custom-call | flops 1073741824 | bytes 4194304 | tf_op jit(solution)/shard_map/pallas_call | solution.py:397
  37.6 0.4 collective-permute-done.2
  38.0 10.0 %all_to_all.22 = f32[32,8,128]{2,1,0:T(8,128)S(1)} all-to-all(f32[32,8,128]{2,1,0:T(8,128)S(1)} %bitcast.23), channel_id=1, replica_groups=mesh['slab'=8,'yz'=4] {'slab','yz'}, dimensions={0} | all-to-all | bytes 262144 | tf_op jit(solution)/shard_map/all_to_all | solution.py:450
  48.0 1.1 %shard_map.127 = (f32[8,4,8,128]{3,2,1,0:T(8,128)S(1)}, f32[2,32,256]{2,1,0:T(8,128)S(1)}) custom-call(f32[8,4,8,128]{3,2,1,0:T(8,128)S(1)} %bitcast.18, bf16[2,32,32,256]{3,2,1,0:T(8,128)(2,1)S(1)} %copy-done.5, bf16[192,128]{1,0:T(8,128)(2,1)S(1)} %copy-done.6, bf16[2,64,128]{2,1,0:T(8,128)(2,1)S(1)} %copy-done.7), custom_call_target="tpu_custom_call" | custom-call | flops 1073741824 | bytes 4194304 | tf_op jit(solution)/shard_map/pallas_call | solution.py:397
  49.1 10.1 %all_to_all.23 = f32[32,8,128]{2,1,0:T(8,128)S(1)} all-to-all(f32[32,8,128]{2,1,0:T(8,128)S(1)} %bitcast.19), channel_id=1, replica_groups=mesh['slab'=8,'yz'=4] {'slab','yz'}, dimensions={0} | all-to-all | bytes 262144 | tf_op jit(solution)/shard_map/all_to_all | solution.py:455
  59.2 0.2 collective-permute-start.3
  59.4 0.2 shard_map.128.product_ref
  59.6 0.9 %collective-permute-done.3.other_ref = f32[8,4,8,128]{3,2,1,0:T(8,128)S(1)} collective-permute-done((f32[8,4,8,128]{3,2,1,0:T(8,128)S(1)}, f32[8,4,8,128]{3,2,1,0:T(8,128)S(1)}, u32[]{:S(2)}, u32[]{:S(2)}) %collective-permute-start.3) | collective-permute-done | bytes 131104 | tf_op jit(solution)/shard_map/ppermute | solution.py:460
  60.5 2.1 %shard_map.129 = (bf16[32,2,64,256]{3,2,1,0:T(8,128)(2,1)}, f32[2,32,32,256]{3,2,1,0:T(8,128)}) custom-call(f32[8,4,8,128]{3,2,1,0:T(8,128)S(1)} %bitcast.15, f32[8,4,8,128]{3,2,1,0:T(8,128)S(1)} %collective-permute-done.3.other_ref, f32[32,2,64,256]{3,2,1,0:T(8,128)S(1)} %shard_map.126.local_ref, bf16[192,256]{1,0:T(8,128)(2,1)S(1)} %get-tuple-element.35.lift_ref, ...), custom_call_target="tpu_custom_call" | custom-call | flops 1073741824 | bytes 4194304 | tf_op jit(solution)/shard_map/pallas_call | solution.py:397
  (12 shorter events, 0.1 us)
Async XLA Ops:
  0.6 3.4 %copy-start = (bf16[32,32]{1,0:T(8,128)(2,1)S(1)}, bf16[32,32]{1,0:T(8,128)(2,1)}, u32[]{:S(2)}) copy-start(bf16[32,32]{1,0:T(8,128)(2,1)} %param.13) | copy-start | bytes 6148
  0.6 3.4 %copy-start.9 = (bf16[256,256]{1,0:T(8,128)(2,1)S(1)}, bf16[256,256]{1,0:T(8,128)(2,1)}, u32[]{:S(2)}) copy-start(bf16[256,256]{1,0:T(8,128)(2,1)} %constant.20.clone) | copy-start | bytes 393220
  0.7 3.4 %copy-start.8 = (bf16[256,32]{1,0:T(8,128)(2,1)S(1)}, bf16[256,32]{1,0:T(8,128)(2,1)}, u32[]{:S(2)}) copy-start(bf16[256,32]{1,0:T(8,128)(2,1)} %constant.19.clone) | copy-start | bytes 49156
  0.7 19.6 %copy-start.6 = (bf16[192,128]{1,0:T(8,128)(2,1)S(1)}, bf16[192,128]{1,0:T(8,128)(2,1)}, u32[]{:S(2)}) copy-start(bf16[192,128]{1,0:T(8,128)(2,1)} %constant.17.clone.refs_2_) | copy-start | bytes 147460
  0.7 19.6 %copy-start.7 = (bf16[2,64,128]{2,1,0:T(8,128)(2,1)S(1)}, bf16[2,64,128]{2,1,0:T(8,128)(2,1)}, u32[]{:S(2)}) copy-start(bf16[2,64,128]{2,1,0:T(8,128)(2,1)} %constant.18.clone.refs_3_) | copy-start | bytes 98308
  0.7 19.6 %copy-start.5 = (bf16[2,32,32,256]{3,2,1,0:T(8,128)(2,1)S(1)}, bf16[2,32,32,256]{3,2,1,0:T(8,128)(2,1)}, u32[]{:S(2)}) copy-start(bf16[2,32,32,256]{3,2,1,0:T(8,128)(2,1)} %refs_1_.3) | copy-start | bytes 3145732
  3.5 1.5 %collective-permute-start = (f32[8,4,8,128]{3,2,1,0:T(8,128)S(1)}, f32[8,4,8,128]{3,2,1,0:T(8,128)S(1)}, u32[]{:S(2)}, u32[]{:S(2)}) collective-permute-start(f32[8,4,8,128]{3,2,1,0:T(8,128)S(1)} %get-tuple-element.27), channel_id=1, source_target_pairs={{0,1},{1,0},{2,3},{3,2},{4,5},{5,4},{6,7},{7,6},{8,9},{9,8},{10,11... | collective-permute-start | bytes 393224 | tf_op jit(solution)/shard_map/ppermute | solution.py:443
  20.3 11.6 %copy-start.1 = (bf16[32,2,64,256]{3,2,1,0:T(8,128)(2,1)S(1)}, bf16[32,2,64,256]{3,2,1,0:T(8,128)(2,1)}, u32[]{:S(2)}) copy-start(bf16[32,2,64,256]{3,2,1,0:T(8,128)(2,1)} %grid_ref.1) | copy-start | bytes 6291460
  31.6 1.4 %copy-start.3 = (bf16[128,256]{1,0:T(8,128)(2,1)S(1)}, bf16[128,256]{1,0:T(8,128)(2,1)}, u32[]{:S(2)}) copy-start(bf16[128,256]{1,0:T(8,128)(2,1)} %constant.22.clone.depth_ref) | copy-start | bytes 196612
  31.6 1.4 %copy-start.4 = (bf16[128,256]{1,0:T(8,128)(2,1)S(1)}, bf16[128,256]{1,0:T(8,128)(2,1)}, u32[]{:S(2)}) copy-start(bf16[128,256]{1,0:T(8,128)(2,1)} %constant.21.clone.synth_ref) | copy-start | bytes 196612
  31.6 1.3 %collective-permute-start.1 = (f32[8,4,8,128]{3,2,1,0:T(8,128)S(1)}, f32[8,4,8,128]{3,2,1,0:T(8,128)S(1)}, u32[]{:S(2)}, u32[]{:S(2)}) collective-permute-start(f32[8,4,8,128]{3,2,1,0:T(8,128)S(1)} %bitcast.16), channel_id=1, source_target_pairs={{0,1},{1,0},{2,3},{3,2},{4,5},{5,4},{6,7},{7,6},{8,9},{9,8},{10,11... | collective-permute-start | bytes 393224 | tf_op jit(solution)/shard_map/ppermute | solution.py:460
  36.6 1.4 %collective-permute-start.2 = (f32[8,4,8,128]{3,2,1,0:T(8,128)S(1)}, f32[8,4,8,128]{3,2,1,0:T(8,128)S(1)}, u32[]{:S(2)}, u32[]{:S(2)}) collective-permute-start(f32[8,4,8,128]{3,2,1,0:T(8,128)S(1)} %get-tuple-element.38), channel_id=1, source_target_pairs={{0,1},{1,0},{2,3},{3,2},{4,5},{5,4},{6,7},{7,6},{8,9},{9,8},{10,11... | collective-permute-start | bytes 393224 | tf_op jit(solution)/shard_map/ppermute | solution.py:443
  49.1 11.4 %copy-start.2 = (bf16[128,256]{1,0:T(8,128)(2,1)S(1)}, bf16[128,256]{1,0:T(8,128)(2,1)}, u32[]{:S(2)}) copy-start(bf16[128,256]{1,0:T(8,128)(2,1)} %constant.23.clone.synth_ref) | copy-start | bytes 196612
  59.2 1.3 %collective-permute-start.3 = (f32[8,4,8,128]{3,2,1,0:T(8,128)S(1)}, f32[8,4,8,128]{3,2,1,0:T(8,128)S(1)}, u32[]{:S(2)}, u32[]{:S(2)}) collective-permute-start(f32[8,4,8,128]{3,2,1,0:T(8,128)S(1)} %bitcast.14), channel_id=1, source_target_pairs={{0,1},{1,0},{2,3},{3,2},{4,5},{5,4},{6,7},{7,6},{8,9},{9,8},{10,11... | collective-permute-start | bytes 393224 | tf_op jit(solution)/shard_map/ppermute | solution.py:460

commit v5 on v4

--- a/solution.py
+++ b/solution.py
@@ -162,9 +162,7 @@
             )
             for e in range(2)
         ]
-        upper, lower = split(jnp.concatenate(lines, axis=0))
-        upper_ref[q, c * groups : (c + 2) * groups] = upper
-        lower_ref[q, c * groups : (c + 2) * groups] = lower
+        upper_ref[q, c * groups : (c + 2) * groups] = jnp.concatenate(lines, axis=0).astype(jnp.bfloat16)
 
 
 def analyze_rows(row_ref, upper_ref, lower_ref, kept_ref, sent_ref):
@@ -173,7 +171,7 @@
     first = lax.axis_index("yz") % 2 == 0
     for q in range(pencils):
         both = dot(row_ref[...], upper_ref[q], 1, 1)
-        total = both[:count] + both[count:] + dot(row_ref[:count], lower_ref[q], 1, 1)
+        total = both[:count] + both[count:]
         low = total[:, :half].reshape(blocks, line, half)
         high = total[:, half:].reshape(blocks, line, half)
         kept_ref[:, q] = jnp.where(first, low, high)

time: 62.8 us -> 62.5 us (level)
  no operation moved by 1% of the time
where the time goes in v5:
time: 62.5 us; the launch traced here: 62.3 us
  blocking collectives  45.3 us (72%)
  Pallas kernels  12.2 us (20%)
  waiting for transfers between devices  2.12 us (3%)
  starting transfers between devices  1.24 us (2%)
  between operations  0.75 us (1%)
    all_to_all x2, blocking collectives, to_owner(): moved = lax.all_to_all(parts, ('slab', 'yz'), 0, 0, tiled=True)  25.2 us
    all_to_all x2, blocking collectives, from_owner(): moved = lax.all_to_all(values, ('slab', 'yz'), 0, 0, tiled=True)  20.1 us
    pallas_call x8, Pallas kernels, call(): pl.pallas_call(kernel, out_shape=outs, in_specs=[HBM if i in far else VME...  12.2 us
    ppermute x2, waiting for transfers between devices, from_owner(): other = lax.ppermute(moved, 'yz', neighbours)  1.32 us
  transfers between devices with their start and end apart: 4, of which 4 were waited for; matrix products, arithmetic and copies ran while one was open for 1% of the time, Pallas kernels for 3%

profile of v5, /device:TPU:0, one launch (start us, length us, event | category | flops | bytes accessed | tf_op | source)
XLA Modules:
  0.0 62.3 jit_solution(2388075073047292106)
XLA Ops:
  0.6 0.0 copy-start
  0.6 0.0 copy-start.9
  0.7 0.0 copy-start.8
  0.7 0.0 copy-start.6
  0.7 0.0 copy-start.7
  0.7 0.0 copy-start.5
  0.7 2.6 %shard_map.122 = (f32[8,4,8,128]{3,2,1,0:T(8,128)S(1)}, f32[8,4,8,128]{3,2,1,0:T(8,128)S(1)}, bf16[128,256]{1,0:T(8,128)(2,1)S(1)}, bf16[192,256]{1,0:T(8,128)(2,1)S(1)}) custom-call(bf16[32,2,64,256]{3,2,1,0:T(8,128)(2,1)} %grid_ref.1, bf16[4,448,256]{2,1,0:T(8,128)(2,1)} %constant.16.clone.table_hbm), custom_call_target="tpu_custom_call" | custom-call | flops 1073741824 | bytes 4194304 | tf_op jit(solution)/shard_map/pallas_call | solution.py:395
  3.3 0.5 collective-permute-start
  3.9 0.3 fusion.1.wide_ref
  4.2 0.3 fusion.wide_ref
  4.5 0.4 collective-permute-done
  4.9 15.2 %all_to_all.20 = f32[32,8,128]{2,1,0:T(8,128)S(1)} all-to-all(f32[32,8,128]{2,1,0:T(8,128)S(1)} %bitcast.22), channel_id=1, replica_groups=mesh['slab'=8,'yz'=4] {'slab','yz'}, dimensions={0} | all-to-all | bytes 262144 | tf_op jit(solution)/shard_map/all_to_all | solution.py:448
  20.1 0.0 copy-done.6
  20.1 0.0 copy-start.1
  20.1 1.3 %shard_map.123 = (f32[8,4,8,128]{3,2,1,0:T(8,128)S(1)}, f32[2,32,256]{2,1,0:T(8,128)S(1)}) custom-call(f32[8,4,8,128]{3,2,1,0:T(8,128)S(1)} %bitcast.20, bf16[2,32,32,256]{3,2,1,0:T(8,128)(2,1)S(1)} %copy-done.5, bf16[192,128]{1,0:T(8,128)(2,1)S(1)} %copy-done.6, bf16[2,64,128]{2,1,0:T(8,128)(2,1)S(1)} %copy-done.7), custom_call_target="tpu_custom_call" | custom-call | flops 1073741824 | bytes 4194304 | tf_op jit(solution)/shard_map/pallas_call | solution.py:395
  21.5 10.0 %all_to_all.21 = f32[32,8,128]{2,1,0:T(8,128)S(1)} all-to-all(f32[32,8,128]{2,1,0:T(8,128)S(1)} %bitcast.21), channel_id=1, replica_groups=mesh['slab'=8,'yz'=4] {'slab','yz'}, dimensions={0} | all-to-all | bytes 262144 | tf_op jit(solution)/shard_map/all_to_all | solution.py:453
  31.5 0.2 collective-permute-start.1
  31.7 0.7 %shard_map.124.local_ref = f32[32,2,64,256]{3,2,1,0:T(8,128)S(1)} custom-call(bf16[32,2,64,256]{3,2,1,0:T(8,128)(2,1)S(1)} %copy-done.1, bf16[256,256]{1,0:T(8,128)(2,1)S(1)} %fusion.wide_ref), custom_call_target="tpu_custom_call" | custom-call | flops 1073741824 | bytes 4194304 | tf_op jit(solution)/shard_map/pallas_call | solution.py:395
  32.4 0.4 collective-permute-done.1.other_ref
  32.8 0.0 copy-done.3
  32.8 3.4 %shard_map.125 = (bf16[32,2,64,256]{3,2,1,0:T(8,128)(2,1)S(1)}, f32[8,4,8,128]{3,2,1,0:T(8,128)S(1)}, f32[8,4,8,128]{3,2,1,0:T(8,128)S(1)}) custom-call(f32[8,4,8,128]{3,2,1,0:T(8,128)S(1)} %bitcast.17, f32[8,4,8,128]{3,2,1,0:T(8,128)S(1)} %collective-permute-done.1.other_ref, f32[32,2,64,256]{3,2,1,0:T(8,128)S(1)} %shard_map.124.local_ref, ...), custom_call_target="tpu_custom_call" | custom-call | flops 1073741824 | bytes 4194304 | tf_op jit(solution)/shard_map/pallas_call | solution.py:395
  36.2 0.3 collective-permute-start.2
  36.5 0.7 %shard_map.126.local_ref = f32[32,2,64,256]{3,2,1,0:T(8,128)S(1)} custom-call(bf16[32,2,64,256]{3,2,1,0:T(8,128)(2,1)S(1)} %get-tuple-element.39.grid_ref, bf16[256,256]{1,0:T(8,128)(2,1)S(1)} %fusion.1.wide_ref), custom_call_target="tpu_custom_call" | custom-call | flops 1073741824 | bytes 4194304 | tf_op jit(solution)/shard_map/pallas_call | solution.py:395
  37.2 0.4 collective-permute-done.2
  37.7 10.0 %all_to_all.22 = f32[32,8,128]{2,1,0:T(8,128)S(1)} all-to-all(f32[32,8,128]{2,1,0:T(8,128)S(1)} %bitcast.23), channel_id=1, replica_groups=mesh['slab'=8,'yz'=4] {'slab','yz'}, dimensions={0} | all-to-all | bytes 262144 | tf_op jit(solution)/shard_map/all_to_all | solution.py:448
  47.7 1.1 %shard_map.127 = (f32[8,4,8,128]{3,2,1,0:T(8,128)S(1)}, f32[2,32,256]{2,1,0:T(8,128)S(1)}) custom-call(f32[8,4,8,128]{3,2,1,0:T(8,128)S(1)} %bitcast.18, bf16[2,32,32,256]{3,2,1,0:T(8,128)(2,1)S(1)} %copy-done.5, bf16[192,128]{1,0:T(8,128)(2,1)S(1)} %copy-done.6, bf16[2,64,128]{2,1,0:T(8,128)(2,1)S(1)} %copy-done.7), custom_call_target="tpu_custom_call" | custom-call | flops 1073741824 | bytes 4194304 | tf_op jit(solution)/shard_map/pallas_call | solution.py:395
  48.8 10.1 %all_to_all.23 = f32[32,8,128]{2,1,0:T(8,128)S(1)} all-to-all(f32[32,8,128]{2,1,0:T(8,128)S(1)} %bitcast.19), channel_id=1, replica_groups=mesh['slab'=8,'yz'=4] {'slab','yz'}, dimensions={0} | all-to-all | bytes 262144 | tf_op jit(solution)/shard_map/all_to_all | solution.py:453
  58.8 0.2 collective-permute-start.3
  59.1 0.2 shard_map.128.product_ref
  59.3 0.9 %collective-permute-done.3.other_ref = f32[8,4,8,128]{3,2,1,0:T(8,128)S(1)} collective-permute-done((f32[8,4,8,128]{3,2,1,0:T(8,128)S(1)}, f32[8,4,8,128]{3,2,1,0:T(8,128)S(1)}, u32[]{:S(2)}, u32[]{:S(2)}) %collective-permute-start.3) | collective-permute-done | bytes 131104 | tf_op jit(solution)/shard_map/ppermute | solution.py:458
  60.2 0.0 copy-done.2
  60.2 2.1 %shard_map.129 = (bf16[32,2,64,256]{3,2,1,0:T(8,128)(2,1)}, f32[2,32,32,256]{3,2,1,0:T(8,128)}) custom-call(f32[8,4,8,128]{3,2,1,0:T(8,128)S(1)} %bitcast.15, f32[8,4,8,128]{3,2,1,0:T(8,128)S(1)} %collective-permute-done.3.other_ref, f32[32,2,64,256]{3,2,1,0:T(8,128)S(1)} %shard_map.126.local_ref, bf16[192,256]{1,0:T(8,128)(2,1)S(1)} %get-tuple-element.35.lift_ref, ...), custom_call_target="tpu_custom_call" | custom-call | flops 1073741824 | bytes 4194304 | tf_op jit(solution)/shard_map/pallas_call | solution.py:395
  (12 shorter events, 0.1 us)
Async XLA Ops:
  0.6 3.2 %copy-start = (bf16[32,32]{1,0:T(8,128)(2,1)S(1)}, bf16[32,32]{1,0:T(8,128)(2,1)}, u32[]{:S(2)}) copy-start(bf16[32,32]{1,0:T(8,128)(2,1)} %param.13) | copy-start | bytes 6148
  0.6 3.2 %copy-start.9 = (bf16[256,256]{1,0:T(8,128)(2,1)S(1)}, bf16[256,256]{1,0:T(8,128)(2,1)}, u32[]{:S(2)}) copy-start(bf16[256,256]{1,0:T(8,128)(2,1)} %constant.20.clone) | copy-start | bytes 393220
  0.7 3.2 %copy-start.8 = (bf16[256,32]{1,0:T(8,128)(2,1)S(1)}, bf16[256,32]{1,0:T(8,128)(2,1)}, u32[]{:S(2)}) copy-start(bf16[256,32]{1,0:T(8,128)(2,1)} %constant.19.clone) | copy-start | bytes 49156
  0.7 19.4 %copy-start.6 = (bf16[192,128]{1,0:T(8,128)(2,1)S(1)}, bf16[192,128]{1,0:T(8,128)(2,1)}, u32[]{:S(2)}) copy-start(bf16[192,128]{1,0:T(8,128)(2,1)} %constant.17.clone.refs_2_) | copy-start | bytes 147460
  0.7 19.4 %copy-start.7 = (bf16[2,64,128]{2,1,0:T(8,128)(2,1)S(1)}, bf16[2,64,128]{2,1,0:T(8,128)(2,1)}, u32[]{:S(2)}) copy-start(bf16[2,64,128]{2,1,0:T(8,128)(2,1)} %constant.18.clone.refs_3_) | copy-start | bytes 98308
  0.7 19.4 %copy-start.5 = (bf16[2,32,32,256]{3,2,1,0:T(8,128)(2,1)S(1)}, bf16[2,32,32,256]{3,2,1,0:T(8,128)(2,1)}, u32[]{:S(2)}) copy-start(bf16[2,32,32,256]{3,2,1,0:T(8,128)(2,1)} %refs_1_.3) | copy-start | bytes 3145732
  3.3 1.5 %collective-permute-start = (f32[8,4,8,128]{3,2,1,0:T(8,128)S(1)}, f32[8,4,8,128]{3,2,1,0:T(8,128)S(1)}, u32[]{:S(2)}, u32[]{:S(2)}) collective-permute-start(f32[8,4,8,128]{3,2,1,0:T(8,128)S(1)} %get-tuple-element.27), channel_id=1, source_target_pairs={{0,1},{1,0},{2,3},{3,2},{4,5},{5,4},{6,7},{7,6},{8,9},{9,8},{10,11... | collective-permute-start | bytes 393224 | tf_op jit(solution)/shard_map/ppermute | solution.py:441
  20.1 11.6 %copy-start.1 = (bf16[32,2,64,256]{3,2,1,0:T(8,128)(2,1)S(1)}, bf16[32,2,64,256]{3,2,1,0:T(8,128)(2,1)}, u32[]{:S(2)}) copy-start(bf16[32,2,64,256]{3,2,1,0:T(8,128)(2,1)} %grid_ref.1) | copy-start | bytes 6291460
  31.5 1.4 %copy-start.3 = (bf16[128,256]{1,0:T(8,128)(2,1)S(1)}, bf16[128,256]{1,0:T(8,128)(2,1)}, u32[]{:S(2)}) copy-start(bf16[128,256]{1,0:T(8,128)(2,1)} %constant.22.clone.depth_ref) | copy-start | bytes 196612
  31.5 1.4 %copy-start.4 = (bf16[128,256]{1,0:T(8,128)(2,1)S(1)}, bf16[128,256]{1,0:T(8,128)(2,1)}, u32[]{:S(2)}) copy-start(bf16[128,256]{1,0:T(8,128)(2,1)} %constant.21.clone.synth_ref) | copy-start | bytes 196612
  31.5 1.3 %collective-permute-start.1 = (f32[8,4,8,128]{3,2,1,0:T(8,128)S(1)}, f32[8,4,8,128]{3,2,1,0:T(8,128)S(1)}, u32[]{:S(2)}, u32[]{:S(2)}) collective-permute-start(f32[8,4,8,128]{3,2,1,0:T(8,128)S(1)} %bitcast.16), channel_id=1, source_target_pairs={{0,1},{1,0},{2,3},{3,2},{4,5},{5,4},{6,7},{7,6},{8,9},{9,8},{10,11... | collective-permute-start | bytes 393224 | tf_op jit(solution)/shard_map/ppermute | solution.py:458
  36.2 1.4 %collective-permute-start.2 = (f32[8,4,8,128]{3,2,1,0:T(8,128)S(1)}, f32[8,4,8,128]{3,2,1,0:T(8,128)S(1)}, u32[]{:S(2)}, u32[]{:S(2)}) collective-permute-start(f32[8,4,8,128]{3,2,1,0:T(8,128)S(1)} %get-tuple-element.38), channel_id=1, source_target_pairs={{0,1},{1,0},{2,3},{3,2},{4,5},{5,4},{6,7},{7,6},{8,9},{9,8},{10,11... | collective-permute-start | bytes 393224 | tf_op jit(solution)/shard_map/ppermute | solution.py:441
  48.8 11.4 %copy-start.2 = (bf16[128,256]{1,0:T(8,128)(2,1)S(1)}, bf16[128,256]{1,0:T(8,128)(2,1)}, u32[]{:S(2)}) copy-start(bf16[128,256]{1,0:T(8,128)(2,1)} %constant.23.clone.synth_ref) | copy-start | bytes 196612
  58.8 1.3 %collective-permute-start.3 = (f32[8,4,8,128]{3,2,1,0:T(8,128)S(1)}, f32[8,4,8,128]{3,2,1,0:T(8,128)S(1)}, u32[]{:S(2)}, u32[]{:S(2)}) collective-permute-start(f32[8,4,8,128]{3,2,1,0:T(8,128)S(1)} %bitcast.14), channel_id=1, source_target_pairs={{0,1},{1,0},{2,3},{3,2},{4,5},{5,4},{6,7},{7,6},{8,9},{9,8},{10,11... | collective-permute-start | bytes 393224 | tf_op jit(solution)/shard_map/ppermute | solution.py:458
